TPU v7x, 32 devices: a whole 2x2x4 slice. The times are simulated.
32 devices in a mesh: vb: 8 (over z, x), vc: 4 (over y, core).
Axes of the slice: x: 2, y: 2, z: 4, core: 2. Of those that a mesh axis runs over, the one named last changes fastest.
Arguments:
- integrals: float32 [2, 512, 512, 512], P(None, 'vb', 'vc'), may hold values from -0.25 to 0.25
- doubles: float32 [3, 512, 512], P(None, 'vb'), may hold values from -6 to 6
- eps_occ: float32 [100], replicated, may hold values from -2 to -0.5
- eps_virt: float32 [512], replicated, may hold values from 0.2 to 3
- triple: int32 [3], replicated, may hold values from 0 to 99
- energy_order: int32 [512], replicated, may hold values from 0 to 511, each once
Outputs:
- amplitudes: float32 [512, 512, 512], P('vb', 'vc')
- grad: float32 [512, 512], P('vb', 'vc')
Inputs may be any that keep to these rules, and one draw needn't show every extreme that they name: `energy_order`: each of 0 to 511 appears once.
All inputs are finite; a program needn't handle non-finite values.
Results may differ from a plain program's by a relative error of at most 0.00007.
Values sent between devices are 32-bit elements; how exact they have to be, the bound alone decides.
No kernel may reach another device: no remote copies, remote signals or barrier semaphores. Data moves between devices by JAX's collectives and lax.ppermute only.
A program may use at most 192 MiB of HBM per device.

v0:
```python
import jax
import jax.numpy as jnp
from jax import lax
from jax.sharding import PartitionSpec as P

V = 512
NOCC = 100


def on_device(integrals, doubles, eps_occ, eps_virt, triple, energy_order):
    highest = lax.Precision.HIGHEST
    all_doubles = lax.all_gather(doubles, "vb", axis=1, tiled=True)
    k_block = integrals[0]
    i_block = integrals[1]
    b_rows = k_block.shape[0]
    c_rows = k_block.shape[1]
    first_term = jnp.einsum("pqd,ad->pqa", k_block, all_doubles[0], precision=highest)
    second_local = jnp.einsum("pqd,bd->bqp", k_block, all_doubles[1], precision=highest)
    second_term = lax.all_to_all(second_local, "vb", split_axis=0, concat_axis=2, tiled=True)
    third_local = jnp.einsum("pqd,cd->pcq", i_block, all_doubles[2], precision=highest)
    third_term = lax.all_to_all(third_local, "vc", split_axis=1, concat_axis=2, tiled=True)
    positions = jnp.arange(V, dtype=jnp.int32)
    one_hot = energy_order[:, None] == positions[None, :]
    virt_energy = jnp.sum(jnp.where(one_hot, eps_virt[None, :], jnp.float32(0.0)), axis=1)
    occ_positions = jnp.arange(NOCC, dtype=jnp.int32)
    occ_hot = triple[:, None] == occ_positions[None, :]
    occ_energy = jnp.sum(jnp.where(occ_hot, eps_occ[None, :], jnp.float32(0.0)))
    b_index = lax.axis_index("vb")
    c_index = lax.axis_index("vc")
    b_energy = lax.dynamic_slice_in_dim(virt_energy, b_index * b_rows, b_rows)
    c_energy = lax.dynamic_slice_in_dim(virt_energy, c_index * c_rows, c_rows)
    denominator = (
        occ_energy - b_energy[:, None, None] - c_energy[None, :, None] - virt_energy[None, None, :]
    )
    amplitudes = (first_term + second_term + third_term) / denominator
    grad_partial = jnp.einsum("bca,bcd->ad", amplitudes, k_block, precision=highest)
    row_sums = lax.psum_scatter(grad_partial, "vb", scatter_dimension=0, tiled=True)
    grad = lax.psum_scatter(row_sums, "vc", scatter_dimension=1, tiled=True)
    return (amplitudes, grad)


def solution(mesh):
    in_specs = (P(None, "vb", "vc", None), P(None, "vb", None), P(), P(), P(), P())
    out_specs = (P("vb", "vc", None), P("vb", "vc"))
    return jax.shard_map(
        on_device, mesh=mesh, in_specs=in_specs, out_specs=out_specs, check_vma=False
    )
```

profile of v0, /device:TPU:0, one launch (start us, length us, event | category | flops | bytes accessed | tf_op | source)
XLA Modules:
  0.0 872.2 jit_solution(8881560929795594256)
XLA Ops:
  7.2 0.0 all-gather.2.cloned.1.call-start
  7.2 0.7 all-gather.2.cloned.1.call-update
  7.9 65.5 %all-gather.2.cloned.1.call-done = f32[3,512,512]{2,1,0:T(8,128)} async-done(((f32[3,64,512]{2,1,0:T(8,128)}), f32[3,512,512]{2,1,0:T(8,128)}) %all-gather.2.cloned.1.call-update) | async-done | bytes 3145744 | tf_op jit(solution)/shard_map/all_gather | solution.py:12
  73.4 31.0 %fusion.17 = f32[64,512,128]{2,1,0:T(8,128)S(1)} fusion(f32[2,64,128,512]{3,2,1,0:T(8,128)} %param.6, f32[3,512,512]{2,1,0:T(8,128)} %all-gather.2.cloned.1.call-done), kind=kOutput, calls=%fused_computation.15 | convolution fusion | flops 25769803776 | bytes 34603008 | tf_op jit(solution)/shard_map/pqd,cd->pcq/dot_general | solution.py:20
  104.4 21.3 %copy.29 = f32[64,512,128]{2,0,1:T(8,128)} copy(f32[64,512,128]{2,1,0:T(8,128)S(1)} %fusion.17) | data formatting | bytes 33554432 | tf_op jit(solution)/shard_map/pqd,cd->pcq/transpose | solution.py:20
  125.7 0.0 copy-start
  125.7 7.5 all-to-all-start.1
  133.2 0.0 copy-done
  133.2 30.7 %fusion.14 = f32[512,128,64]{1,0,2:T(8,128)S(1)} fusion(f32[2,64,128,512]{3,2,1,0:T(8,128)} %param.6, f32[3,512,512]{2,1,0:T(8,128)S(1)} %copy-done), kind=kOutput, calls=%fused_computation.14 | convolution fusion | flops 25769803776 | bytes 34603008 | tf_op jit(solution)/shard_map/pqd,bd->bqp/dot_general | solution.py:18
  163.9 21.4 %copy.26 = f32[512,128,64]{1,2,0:T(8,128)} copy(f32[512,128,64]{1,0,2:T(8,128)S(1)} %fusion.14) | data formatting | bytes 33554432 | tf_op jit(solution)/shard_map/pqd,bd->bqp/transpose | solution.py:18
  185.4 0.0 copy-start.1
  185.4 0.0 copy-start.2
  185.4 0.0 copy-start.3
  185.4 0.0 copy-start.4
  185.4 130.8 %all-to-all-done.1 = f32[64,512,128]{2,0,1:T(8,128)} async-done(((f32[64,512,128]{2,0,1:T(8,128)}), f32[64,512,128]{2,0,1:T(8,128)}, u32[]{:S(2)}, u32[]{:S(2)}) %all-to-all-start.1) | async-done | bytes 16777248 | tf_op jit(solution)/shard_map/all_to_all | solution.py:21
  316.2 5.8 all-to-all-start
  322.0 0.0 reduce-scatter.3.cloned.1.call-start
  322.1 0.0 copy-done.1
  322.1 0.0 copy-done.2
  322.1 0.2 select_reduce_fusion
  322.3 0.1 dynamic_slice.7
  322.4 0.0 copy-done.3
  322.4 0.0 copy-done.4
  322.4 0.7 select_reduce_fusion.1
  323.1 0.7 dynamic-slice_subtract_fusion
  323.8 0.1 broadcast_subtract_fusion
  323.9 21.0 %copy.34 = f32[64,4,128,128]{3,1,2,0:T(4,128)} copy(f32[64,4,128,128]{3,0,2,1:T(8,128)} %bitcast.13) | data formatting | bytes 33554432 | tf_op jit(solution)/shard_map/all_to_all | solution.py:21
  344.9 19.9 %all_to_all.33 = f32[64,128,512]{2,1,0:T(8,128)} reshape(f32[64,128,4,128]{3,2,1,0:T(4,128)} %bitcast.61) | data formatting | bytes 33554432 | tf_op jit(solution)/shard_map/all_to_all | solution.py:21
  364.8 320.1 %all-to-all-done = f32[512,128,64]{1,2,0:T(8,128)} async-done(((f32[512,128,64]{1,2,0:T(8,128)}), f32[512,128,64]{1,2,0:T(8,128)}, u32[]{:S(2)}, u32[]{:S(2)}) %all-to-all-start) | async-done | bytes 16777248 | tf_op jit(solution)/shard_map/all_to_all | solution.py:19
  684.9 12.0 %copy.27 = f32[64,128,8,64]{1,3,2,0:T(8,128)} copy(f32[64,128,8,64]{1,3,0,2:T(8,128)} %bitcast.7) | data formatting | bytes 33554432 | tf_op jit(solution)/shard_map/all_to_all | solution.py:19
  696.9 17.4 %copy.28 = f32[64,128,512]{2,1,0:T(8,128)} copy(f32[64,128,512]{1,2,0:T(8,128)} %bitcast.62) | data formatting | bytes 33554432 | tf_op jit(solution)/shard_map/all_to_all | solution.py:19
  714.3 35.8 %subtract_divide_fusion = f32[64,128,512]{2,1,0:T(8,128)} fusion(f32[64,128,512]{2,1,0:T(8,128)} %all_to_all.33, f32[64,128,512]{2,1,0:T(8,128)} %copy.28, f32[2,64,128,512]{3,2,1,0:T(8,128)} %param.6, f32[512]{0:T(512)S(1)} %select_reduce_fusion, f32[64,128]{1,0:T(8,128)S(1)} %broadcast_subtract_fusion, f32[3,512,512]{2,1,0:T(8,128)S(1)} %copy-done), kind=kOutput, calls=%fused_computation.9 | convolution fusion | flops 25786580992 | bytes 68192256 | tf_op jit(solution)/shard_map/pqd,ad->pqa/dot_general | solution.py:17
  750.1 31.8 %fusion.20 = f32[512,512]{1,0:T(8,128)} fusion(f32[64,128,512]{2,1,0:T(8,128)} %subtract_divide_fusion, f32[2,64,128,512]{3,2,1,0:T(8,128)} %param.6), kind=kOutput, calls=%fused_computation.16 | convolution fusion | flops 25769803776 | bytes 34603008 | tf_op jit(solution)/shard_map/bca,bcd->ad/dot_general | solution.py:36
  781.9 0.0 reduce-scatter.3.cloned.1.call-update
  781.9 0.0 reduce-scatter.5.cloned.1.call-start
  782.0 61.7 %reduce-scatter.3.cloned.1.call-done = f32[64,512]{1,0:T(8,128)} async-done(((f32[512,512]{1,0:T(8,128)}), f32[64,512]{1,0:T(8,128)}) %reduce-scatter.3.cloned.1.call-update) | async-done | bytes 131088 | tf_op jit(solution)/shard_map/reduce_scatter | solution.py:37
  843.7 0.0 reduce-scatter.5.cloned.1.call-update
  843.7 21.8 %reduce-scatter.5.cloned.1.call-done = f32[64,128]{1,0:T(8,128)} async-done(((f32[64,512]{1,0:T(8,128)}), f32[64,128]{1,0:T(8,128)}) %reduce-scatter.5.cloned.1.call-update) | async-done | bytes 32784 | tf_op jit(solution)/shard_map/reduce_scatter | solution.py:38
Async XLA Ops:
  7.2 66.3 %all-gather.2.cloned.1.call-start = ((), (), s32[]{:S(2)}) async-start(), calls=%async_computation.4 | async-start | bytes 3538944 | tf_op jit(solution)/shard_map/all_gather | solution.py:12
  125.7 7.5 copy-start
  125.7 190.5 %all-to-all-start.1 = ((f32[64,512,128]{2,0,1:T(8,128)}), f32[64,512,128]{2,0,1:T(8,128)}, u32[]{:S(2)}, u32[]{:S(2)}) async-start(f32[64,512,128]{2,0,1:T(8,128)} %copy.29), calls=%async_computation.1 | async-start | bytes 33554432 | tf_op jit(solution)/shard_map/all_to_all | solution.py:21
  185.4 136.7 %copy-start.1 = (f32[512]{0:T(512)S(1)}, f32[512]{0:T(512)}, u32[]{:S(2)}) copy-start(f32[512]{0:T(512)} %param.9) | copy-start | bytes 6148
  185.4 136.7 %copy-start.2 = (s32[512]{0:T(512)S(1)}, s32[512]{0:T(512)}, u32[]{:S(2)}) copy-start(s32[512]{0:T(512)} %param.11) | copy-start | bytes 6148
  185.4 137.0 %copy-start.3 = (f32[100]{0:T(128)S(1)}, f32[100]{0:T(128)}, u32[]{:S(2)}) copy-start(f32[100]{0:T(128)} %param.8) | copy-start | bytes 1204
  185.4 137.0 %copy-start.4 = (s32[3]{0:T(128)S(1)}, s32[3]{0:T(128)}, u32[]{:S(2)}) copy-start(s32[3]{0:T(128)} %param.10) | copy-start | bytes 40
  316.2 368.7 %all-to-all-start = ((f32[512,128,64]{1,2,0:T(8,128)}), f32[512,128,64]{1,2,0:T(8,128)}, u32[]{:S(2)}, u32[]{:S(2)}) async-start(f32[512,128,64]{1,2,0:T(8,128)} %copy.26), calls=%async_computation | async-start | bytes 33554432 | tf_op jit(solution)/shard_map/all_to_all | solution.py:19
  322.0 521.7 %reduce-scatter.3.cloned.1.call-start = ((), (), s32[]{:S(2)}) async-start(), calls=%async_computation.5 | async-start | bytes 1179648 | tf_op jit(solution)/shard_map/reduce_scatter | solution.py:37
  781.9 83.6 %reduce-scatter.5.cloned.1.call-start = ((), (), s32[]{:S(2)}) async-start(), calls=%async_computation.6 | async-start | bytes 163840 | tf_op jit(solution)/shard_map/reduce_scatter | solution.py:38
Sparse Core Ops, SparseCore 0:
  10.2 63.1 all-gather.1
  782.0 61.6 reduce-scatter.2
  846.8 18.5 reduce-scatter.4
where the time goes:
time: 879 us; the launch traced here: 872 us
  waiting for transfers between devices  601 us (68%)
  matrix products  129 us (15%)
  local copies, waits for them, and re-layouts  113 us (13%)
  between operations  14 us (2%)
  starting transfers between devices  13.4 us (2%)
    all_to_all x1, waiting for transfers between devices, on_device(): lax.all_to_all(second_local, 'vb', split_axis=0, concat_axis=2, tiled=True)  320 us
    all_to_all x1, waiting for transfers between devices, on_device(): lax.all_to_all(third_local, 'vc', split_axis=1, concat_axis=2, tiled=True)  131 us
    all_gather x1, waiting for transfers between devices, on_device(): all_doubles = lax.all_gather(doubles, 'vb', axis=1, tiled=True)  65.5 us
    reduce_scatter x1, waiting for transfers between devices, on_device(): lax.psum_scatter(grad_partial, 'vb', scatter_dimension=0, tiled=True)  61.7 us
    all_to_all x2, local copies, waits for them, and re-layouts, on_device(): lax.all_to_all(third_local, 'vc', split_axis=1, concat_axis=2, tiled=True)  40.9 us
    dot_general x1, matrix products, on_device(): jnp.einsum('pqd,ad->pqa', k_block, all_doubles[0], precision=highest)  35.8 us
    dot_general x1, matrix products, on_device(): jnp.einsum('bca,bcd->ad', amplitudes, k_block, precision=highest)  31.8 us
    dot_general x1, matrix products, on_device(): jnp.einsum('pqd,cd->pcq', i_block, all_doubles[2], precision=highest)  31 us
  transfers between devices with their start and end apart: 5, of which 5 were waited for; matrix products, arithmetic and copies ran while one was open for 9% of the time, Pallas kernels for 0%

commit v1 on v0

v1 whole, which is shorter than its diff:
```python
import functools

import jax
import jax.numpy as jnp
from jax import lax
from jax.experimental import pallas as pl
from jax.experimental.pallas import tpu as pltpu
from jax.sharding import PartitionSpec as P

F32 = jnp.float32
BF16 = jnp.bfloat16
NT = (((1,), (1,)), ((), ()))
NN = (((1,), (0,)), ((), ()))
LANES = 128
WIDE = 256
SHARE = 1000
VMEM_BYTES = 48 * 1024 * 1024


def split(x):
    head = x.astype(BF16)
    return head, (x - head.astype(F32)).astype(BF16)


def dot3(both, right, dims):
    rows = both.shape[0] // 2

    def dot(a, b):
        return lax.dot_general(a, b, dims, preferred_element_type=F32)

    main = dot(both, right[0])
    return main[:rows] + (main[rows:] + dot(both[:rows], right[1]))


def stack(x):
    return jnp.concatenate(split(x), axis=0)


def params(cost_flops, cost_bytes):
    return dict(
        compiler_params=pltpu.CompilerParams(
            dimension_semantics=("arbitrary",), vmem_limit_bytes=VMEM_BYTES
        ),
        cost_estimate=pl.CostEstimate(
            flops=cost_flops // SHARE, bytes_accessed=cost_bytes // SHARE, transcendentals=0
        ),
    )


def second_kernel(peers, tile, per_dot, k_ref, *refs):
    count = (len(refs) - 2) // 2
    d_refs, out_refs = refs[:count], refs[count : 2 * count]
    rows, both = refs[2 * count :]
    nc = k_ref.shape[2]
    depth = k_ref.shape[3]
    width = both.shape[0] // 2
    starts = [sum(d.shape[0] for d in d_refs[:q]) for q in range(count)]

    @pl.when(pl.program_id(0) == 0)
    def _():
        for d_ref, at in zip(d_refs, starts):
            h, t = split(d_ref[...])
            both[at : at + d_ref.shape[0], :] = h
            both[width + at : width + at + d_ref.shape[0], :] = t

    left = both[...]
    for p in range(0, tile, per_dot):
        kk = split(k_ref[0, p : p + per_dot].reshape(per_dot * nc, depth))
        r = dot3(left, kk, NT)
        for s in range(per_dot):
            rows[(p + s) * width : (p + s + 1) * width, :] = r[:, s * nc : (s + 1) * nc]
    for out_ref, at in zip(out_refs, starts):
        nb = out_ref.shape[1]
        for peer in range(peers):
            for b in range(nb):
                from_row = at + peer * nb + b
                out_ref[peer, b, :, :] = rows[pl.ds(from_row, tile, stride=width), :]


def second(integrals, d_rows, peers):
    heights = tuple(d.shape[0] for d in d_rows)
    width = sum(heights)
    na, nc, depth = integrals.shape[1:]
    tile = 8
    per_dot = max(1, WIDE // nc)
    flops = 6 * width * na * nc * depth
    size = 4 * (na * nc * depth + width * na * nc)
    return pl.pallas_call(
        functools.partial(second_kernel, peers, tile, per_dot),
        grid=(na // tile,),
        in_specs=[pl.BlockSpec((1, tile, nc, depth), lambda s: (0, s, 0, 0))]
        + [pl.BlockSpec((h, depth), lambda s: (0, 0)) for h in heights],
        out_specs=[
            pl.BlockSpec((peers, h // peers, tile, nc), lambda s: (0, 0, s, 0)) for h in heights
        ],
        out_shape=[jax.ShapeDtypeStruct((peers, h // peers, na, nc), F32) for h in heights],
        scratch_shapes=[
            pltpu.VMEM((tile * width, nc), F32),
            pltpu.VMEM((2 * width, depth), BF16),
        ],
        name="second",
        **params(flops, size),
    )(integrals, *d_rows)


def third_kernel(i_ref, d_ref, *refs):
    out_refs, (head, tail) = refs[:-2], refs[-2:]
    tile, na, depth = i_ref.shape[1:]
    nc = out_refs[0].shape[2]

    @pl.when(pl.program_id(0) == 0)
    def _():
        h, t = split(d_ref[...].T)
        head[...] = h
        tail[...] = t

    r = dot3(stack(i_ref[0].reshape(tile * na, depth)), (head[...], tail[...]), NN)
    for q, out_ref in enumerate(out_refs):
        out_ref[...] = r[:, q * nc : (q + 1) * nc].reshape(tile, na, nc)


def third(integrals, d_rows, blocks):
    nb, na, depth = integrals.shape[1:]
    total = d_rows.shape[0]
    nc = total // blocks
    tile = 4
    flops = 6 * nb * na * total * depth
    size = 4 * (nb * na * depth + nb * na * total)
    return pl.pallas_call(
        third_kernel,
        grid=(nb // tile,),
        in_specs=[
            pl.BlockSpec((1, tile, na, depth), lambda s: (1, s, 0, 0)),
            pl.BlockSpec((total, depth), lambda s: (0, 0)),
        ],
        out_specs=[pl.BlockSpec((tile, na, nc), lambda s: (s, 0, 0))] * blocks,
        out_shape=[jax.ShapeDtypeStruct((nb, na, nc), F32)] * blocks,
        scratch_shapes=[pltpu.VMEM((depth, total), BF16)] * 2,
        name="third",
        **params(flops, size),
    )(integrals, d_rows)


def first_kernel(per_dot, off_ref, k_ref, d_ref, *refs):
    r_refs = refs[:-2]
    out_ref, both = refs[-2:]
    tile, nc, depth = k_ref.shape[1:]
    na = r_refs[0].shape[1]

    @pl.when(pl.program_id(0) == 0)
    def _():
        both[...] = stack(d_ref[...])

    left = both[...]
    for p in range(0, tile, per_dot):
        kk = split(k_ref[0, p : p + per_dot].reshape(per_dot * nc, depth))
        r = dot3(left, kk, NT)
        for s in range(per_dot):
            out_ref[p + s, :, :] = r[:, s * nc : (s + 1) * nc]
    for q, r_ref in enumerate(r_refs):
        at = pl.ds(pl.multiple_of(off_ref[q], na), na)
        for b in range(tile):
            out_ref[b, at, :] += r_ref[b]


def first(integrals, d_rows, offsets, thirds):
    nb, nc, depth = integrals.shape[1:]
    total = d_rows.shape[0]
    na = thirds[0].shape[1]
    per_dot = max(1, WIDE // nc)
    tile = 2 * per_dot
    flops = 6 * nb * nc * total * depth
    size = 4 * (nb * nc * depth + 2 * nb * nc * total)
    return pl.pallas_call(
        functools.partial(first_kernel, per_dot),
        grid_spec=pltpu.PrefetchScalarGridSpec(
            num_scalar_prefetch=1,
            grid=(nb // tile,),
            in_specs=[
                pl.BlockSpec((1, tile, nc, depth), lambda s, o: (0, s, 0, 0)),
                pl.BlockSpec((total, depth), lambda s, o: (0, 0)),
            ]
            + [pl.BlockSpec((tile, na, nc), lambda s, o: (s, 0, 0)) for _ in thirds],
            out_specs=pl.BlockSpec((tile, total, nc), lambda s, o: (s, 0, 0)),
            scratch_shapes=[pltpu.VMEM((2 * total, depth), BF16)],
        ),
        out_shape=jax.ShapeDtypeStruct((nb, total, nc), F32),
        name="first",
        **params(flops, size),
    )(offsets, integrals, d_rows, *thirds)


def finish_kernel(b0, eb_ref, ec_ref, ea_ref, k_ref, q_ref, t_ref, *refs):
    out_ref, grad_ref = refs[-2:]
    tile, nc, depth = k_ref.shape[1:]
    peers, _, na, _ = t_ref.shape
    step = pl.program_id(0)

    @pl.when(step == 0)
    def _():
        grad_ref[...] = refs[1][...] if len(refs) == 4 else jnp.zeros_like(grad_ref)

    amps = []
    for b in range(tile):
        num = t_ref[:, b].reshape(peers * na, nc) + q_ref[b]
        amp = num / ((eb_ref[b0 + step * tile + b] - ec_ref[...]) - ea_ref[...])
        out_ref[b, :, :] = amp.T
        amps.append(amp)
    left = stack(jnp.concatenate(amps, axis=1))
    kk = split(k_ref[0].reshape(tile * nc, depth))
    r = dot3(left, kk, NN)
    for q in range(grad_ref.shape[0]):
        grad_ref[q] += r[:, q * nc : (q + 1) * nc]


def finish(integrals, base, blocks, eb, ec, ea, b0, given):
    nc, depth = integrals.shape[2:]
    peers, nb, na, _ = blocks.shape
    total = peers * na
    tile = 2 * max(1, WIDE // nc)
    at = b0 // tile
    flops = 6 * nb * nc * total * depth
    size = 4 * (nb * nc * depth + 3 * nb * nc * total)
    return pl.pallas_call(
        functools.partial(finish_kernel, b0),
        grid_spec=pltpu.PrefetchScalarGridSpec(
            num_scalar_prefetch=1,
            grid=(nb // tile,),
            in_specs=[
                pl.BlockSpec((1, nc), lambda s, e: (0, 0)),
                pl.BlockSpec((total, nc), lambda s, e: (0, 0)),
                pl.BlockSpec((1, tile, nc, depth), lambda s, e: (0, s + at, 0, 0)),
                pl.BlockSpec((tile, total, nc), lambda s, e: (s + at, 0, 0)),
                pl.BlockSpec((peers, tile, na, nc), lambda s, e: (0, s, 0, 0)),
            ]
            + [
                pl.BlockSpec(memory_space=pl.ANY),
                pl.BlockSpec((depth // nc, total, nc), lambda s, e: (0, 0, 0)),
            ][: len(given)],
            out_specs=[
                pl.BlockSpec((tile, nc, total), lambda s, e: (s + at, 0, 0)),
                pl.BlockSpec((depth // nc, total, nc), lambda s, e: (0, 0, 0)),
            ],
        ),
        out_shape=[
            jax.ShapeDtypeStruct((base.shape[0], nc, total), F32),
            jax.ShapeDtypeStruct((depth // nc, total, nc), F32),
        ],
        input_output_aliases={6: 0} if given else {},
        name="finish",
        **params(flops, size),
    )(eb, ec, ea, integrals, base, blocks, *given)


def energies(eps_occ, eps_virt, triple, energy_order):
    positions = jnp.arange(eps_virt.shape[0], dtype=jnp.int32)
    one_hot = energy_order[:, None] == positions[None, :]
    virt = jnp.sum(jnp.where(one_hot, eps_virt[None, :], F32(0.0)), axis=1)
    occ_positions = jnp.arange(eps_occ.shape[0], dtype=jnp.int32)
    occ_hot = triple[:, None] == occ_positions[None, :]
    occ = jnp.sum(jnp.where(occ_hot, eps_occ[None, :], F32(0.0)))
    return virt, occ


def tie(value, *after):
    return lax.optimization_barrier((value, after))[0]


def in_blocks(n, m, integrals, doubles, eps_occ, eps_virt, triple, energy_order):
    nb, nc, total = integrals.shape[1:]
    i = lax.axis_index("vb")
    j = lax.axis_index("vc")
    depth = total

    def over_b(x, k):
        return lax.ppermute(x, "vb", [(p, p ^ k) for p in range(n)]) if k else x

    def over_c(x, k):
        return lax.ppermute(x, "vc", [(p, p ^ k) for p in range(m)]) if k else x

    def all_over_b(x):
        return lax.all_to_all(x, "vb", split_axis=0, concat_axis=0, tiled=True)

    def in_order(pieces, place, axis):
        x = jnp.stack(pieces)
        ordered = [
            lax.dynamic_index_in_dim(x, place ^ p, 0, False) for p in range(len(pieces))
        ]
        return jnp.concatenate(ordered, axis=axis)

    lots = [nb // 4, nb - nb // 4 - nb // 8, nb // 8]
    starts = [0, lots[0], lots[0] + lots[1]]

    own = doubles[1][: lots[0]]
    rows = in_order([over_b(own, k) for k in range(n)], i, 0)
    (lot,) = second(integrals, (rows,), n)

    share = depth // m
    part = lax.dynamic_slice_in_dim(tie(doubles, rows), j * share, share, axis=2)
    part = jnp.stack([over_b(part, k) for k in range(0, n, 2)])
    part = jnp.stack([part, over_b(part, 1)], axis=1).reshape((n,) + part.shape[1:])
    part = in_order([part[k] for k in range(n)], i, 1)
    arrived = [all_over_b(tie(lot, part))]
    full = in_order([over_c(part, q) for q in range(m)], j, 2)

    d2 = jnp.concatenate([lax.dynamic_slice_in_dim(full[2], (j ^ q) * nc, nc) for q in range(m)])
    thirds = third(integrals, d2, m)

    by_peer = full[1].reshape(n, nb, depth)
    rows = [
        by_peer[:, at : at + lot].reshape(n * lot, depth)
        for at, lot in zip(starts[1:], lots[1:])
    ]
    made = second(integrals, tie(tuple(rows), *thirds), n)
    thirds = [over_c(x, q) for q, x in enumerate(thirds)]
    made = tie(tuple(made), arrived[0])
    arrived.append(all_over_b(made[0]))

    virt, occ = energies(eps_occ, eps_virt, triple, energy_order)
    eb = occ - lax.dynamic_slice_in_dim(virt, i * nb, nb)
    ec = lax.dynamic_slice_in_dim(virt, j * nc, nc)[None, :]
    ea = jnp.broadcast_to(virt[:, None], (total, nc))
    offsets = jnp.stack([(j ^ q) * nc for q in range(m)]).astype(jnp.int32)
    base = first(integrals, full[0], offsets, thirds)

    given = finish(integrals, base, arrived[0], eb, ec, ea, starts[0], ())
    arrived.append(all_over_b(tie(made[1], arrived[1], given[1])))
    for blocks, at in zip(arrived[1:], starts[1:]):
        given = finish(integrals, base, blocks, eb, ec, ea, at, given)
    amplitudes, grad = given

    step = 1
    while step < m:
        bit = (j // step) % 2
        pairs = grad.reshape(-1, 2, total, nc)
        keep = lax.dynamic_index_in_dim(pairs, bit, 1, False)
        give = lax.dynamic_index_in_dim(pairs, 1 - bit, 1, False)
        grad = keep + over_c(give, step)
        step *= 2
    grad = grad.reshape(total, nc)

    grad = sum(
        over_b(lax.dynamic_slice_in_dim(grad, (i ^ k) * nb, nb), k) for k in range(n)
    )
    return amplitudes, grad


def plain(integrals, doubles, eps_occ, eps_virt, triple, energy_order):
    highest = lax.Precision.HIGHEST
    all_doubles = lax.all_gather(doubles, "vb", axis=1, tiled=True)
    k_block = integrals[0]
    i_block = integrals[1]
    nb, nc = k_block.shape[:2]
    first_term = jnp.einsum("pqd,ad->pqa", k_block, all_doubles[0], precision=highest)
    second_local = jnp.einsum("pqd,bd->bqp", k_block, all_doubles[1], precision=highest)
    second_term = lax.all_to_all(second_local, "vb", split_axis=0, concat_axis=2, tiled=True)
    third_local = jnp.einsum("pqd,cd->pcq", i_block, all_doubles[2], precision=highest)
    third_term = lax.all_to_all(third_local, "vc", split_axis=1, concat_axis=2, tiled=True)
    virt, occ = energies(eps_occ, eps_virt, triple, energy_order)
    eb = lax.dynamic_slice_in_dim(virt, lax.axis_index("vb") * nb, nb)
    ec = lax.dynamic_slice_in_dim(virt, lax.axis_index("vc") * nc, nc)
    low = occ - eb[:, None, None] - ec[None, :, None] - virt[None, None, :]
    amplitudes = (first_term + second_term + third_term) / low
    partial = jnp.einsum("bca,bcd->ad", amplitudes, k_block, precision=highest)
    rows = lax.psum_scatter(partial, "vb", scatter_dimension=0, tiled=True)
    grad = lax.psum_scatter(rows, "vc", scatter_dimension=1, tiled=True)
    return amplitudes, grad


def on_device(n, m, *args):
    nb, nc, total = args[0].shape[1:]
    power = n & (n - 1) == 0 and m & (m - 1) == 0
    fits = nc % LANES == 0 and nb % 32 == 0
    if power and fits:
        return in_blocks(n, m, *args)
    return plain(*args)


def solution(mesh):
    n, m = mesh.shape["vb"], mesh.shape["vc"]
    in_specs = (P(None, "vb", "vc", None), P(None, "vb", None), P(), P(), P(), P())
    out_specs = (P("vb", "vc", None), P("vb", "vc"))
    return jax.shard_map(
        functools.partial(on_device, n, m),
        mesh=mesh,
        in_specs=in_specs,
        out_specs=out_specs,
        check_vma=False,
    )
```

time: 879 us -> 458 us (0.52)
  waiting for transfers between devices: 601 us -> 272 us
  matrix products: 129 us -> 0 us
  Pallas kernels: 0 us -> 117 us
  local copies, waits for them, and re-layouts: 113 us -> 14.5 us
  starting transfers between devices: 13.4 us -> 48.1 us
  between operations: 14 us -> 1.06 us
    all_to_all x2 -> x3, waiting for transfers between devices: 451 us -> 36.4 us  [all_over_b(): return lax.all_to_all(x, 'vb', split_axis=0, concat_axis=0, tiled=True)]
    ppermute x0 -> x26, waiting for transfers between devices: none -> 235 us  [the longest x8 223 us: over_c(): return lax.ppermute(x, 'vc', [(p, p ^ k) for p in range(m)]) if k else x]
    dot_general x4 -> x0, matrix products: 129 us -> none  [the longest x1 35.8 us: on_device(): jnp.einsum('pqd,ad->pqa', k_block, all_doubles[0], precision=highest)]
    pallas_call x0 -> x7, Pallas kernels: none -> 117 us  [the longest x3 34.4 us: finish(): pl.pallas_call(functools.partial(finish_kernel, b0), grid_spec=pltpu.Pref...]
    reduce_scatter x2 -> x0, waiting for transfers between devices: 83.5 us -> none  [the longest x1 61.7 us: on_device(): lax.psum_scatter(grad_partial, 'vb', scatter_dimension=0, tiled=True)]
    all_to_all x4 -> x0, local copies, waits for them, and re-layouts: 70.4 us -> none  [the longest x2 40.9 us: on_device(): lax.all_to_all(third_local, 'vc', split_axis=1, concat_axis=2, tiled=True)]
    all_gather x1 -> x0, waiting for transfers between devices: 65.5 us -> none  [on_device(): all_doubles = lax.all_gather(doubles, 'vb', axis=1, tiled=True)]
    transpose x2 -> x0, local copies, waits for them, and re-layouts: 42.7 us -> none  [the longest x1 21.4 us: on_device(): jnp.einsum('pqd,bd->bqp', k_block, all_doubles[1], precision=highest)]
  transfers between devices with their start and end apart: 5 -> 29, of which waited for: 5 -> 18; matrix products, arithmetic and copies ran while one was open for 9% -> 1% of each run, Pallas kernels for 0% -> 25%
where the time goes in v1:
time: 458 us; the launch traced here: 456 us
  waiting for transfers between devices  272 us (59%)
  Pallas kernels  117 us (26%)
  starting transfers between devices  48.1 us (11%)
  local copies, waits for them, and re-layouts  14.5 us (3%)
    ppermute x8, waiting for transfers between devices, over_c(): return lax.ppermute(x, 'vc', [(p, p ^ k) for p in range(m)]) if k else x  223 us
    all_to_all x3, waiting for transfers between devices, all_over_b(): return lax.all_to_all(x, 'vb', split_axis=0, concat_axis=0, tiled=True)  36.4 us
    pallas_call x3, Pallas kernels, finish(): pl.pallas_call(functools.partial(finish_kernel, b0), grid_spec=pltpu.Pref...  34.4 us
    pallas_call x2, Pallas kernels, second(): pl.pallas_call(functools.partial(second_kernel, peers, tile, per_dot), gr...  33.6 us
    ppermute x18, starting transfers between devices, over_b(): return lax.ppermute(x, 'vb', [(p, p ^ k) for p in range(n)]) if k else x  28.9 us
    pallas_call x1, Pallas kernels, first(): pl.pallas_call(functools.partial(first_kernel, per_dot), grid_spec=pltpu....  26.7 us
    pallas_call x1, Pallas kernels, third(): pl.pallas_call(third_kernel, grid=(nb // tile,), in_specs=[pl.BlockSpec((...  22.4 us
    all_to_all x3, starting transfers between devices, all_over_b(): return lax.all_to_all(x, 'vb', split_axis=0, concat_axis=0, tiled=True)  13.7 us
  transfers between devices with their start and end apart: 29, of which 18 were waited for; matrix products, arithmetic and copies ran while one was open for 1% of the time, Pallas kernels for 25%

profile of v1, /device:TPU:0, one launch (start us, length us, event | category | flops | bytes accessed | tf_op | source)
XLA Modules:
  0.0 456.5 jit_solution(850894231055531395)
XLA Ops:
  1.4 2.9 collective-permute-start
  4.3 1.6 collective-permute-start.1
  5.9 3.0 collective-permute-start.3
  8.9 1.3 collective-permute-start.4
  10.2 3.6 collective-permute-start.5
  13.9 0.9 collective-permute-done.4
  14.8 1.2 collective-permute-done.5
  16.0 4.4 collective-permute-done.6
  21.7 4.2 collective-permute-start.7
  26.8 1.3 collective-permute-done.9
  28.0 1.4 collective-permute-done.8
  30.4 12.4 %second.3 = f32[8,16,64,128]{3,2,1,0:T(8,128)S(1)} custom-call(f32[2,64,128,512]{3,2,1,0:T(8,128)} %k_ref.11, f32[128,512]{1,0:T(8,128)S(1)} %constant_dynamic-update-slice_fusion.8.refs_0_), custom_call_target="tpu_custom_call" | custom-call | flops 3221225 | bytes 20971 | tf_op jit(solution)/shard_map/second/pallas_call | solution.py:88
  42.8 1.9 copy-done
  45.0 4.6 %all-to-all-start = ((f32[8,16,64,128]{3,2,1,0:T(8,128)}), f32[8,16,64,128]{3,2,1,0:T(8,128)}, u32[]{:S(2)}, u32[]{:S(2)}) async-start(f32[8,16,64,128]{3,2,1,0:T(8,128)} %copy-done), calls=%async_computation | async-start | bytes 8388608 | tf_op jit(solution)/shard_map/all_to_all | solution.py:282
  49.7 1.6 collective-permute-start.12
  51.5 17.9 %collective-permute-done.13 = f32[3,512,128]{2,1,0:T(8,128)S(1)} collective-permute-done((f32[3,512,128]{2,1,0:T(8,128)S(1)}, f32[3,512,128]{2,1,0:T(8,128)S(1)}, u32[]{:S(2)}, u32[]{:S(2)}) %collective-permute-start.13) | collective-permute-done | bytes 786464 | tf_op jit(solution)/shard_map/ppermute | solution.py:279
  69.5 16.9 %collective-permute-done.12 = f32[3,512,128]{2,1,0:T(8,128)S(1)} collective-permute-done((f32[3,512,128]{2,1,0:T(8,128)S(1)}, f32[3,512,128]{2,1,0:T(8,128)S(1)}, u32[]{:S(2)}, u32[]{:S(2)}) %collective-permute-start.12) | collective-permute-done | bytes 786464 | tf_op jit(solution)/shard_map/ppermute | solution.py:279
  87.6 22.4 %third.1 = (f32[64,128,128]{2,1,0:T(8,128)S(1)}, f32[64,128,128]{2,1,0:T(8,128)}, f32[64,128,128]{2,1,0:T(8,128)}, f32[64,128,128]{2,1,0:T(8,128)}) custom-call(f32[2,64,128,512]{3,2,1,0:T(8,128)} %k_ref.11, f32[512,512]{1,0:T(8,128)S(1)} %pad_maximum_fusion.2.d_ref), custom_call_target="tpu_custom_call" | custom-call | flops 12884901 | bytes 33554 | tf_op jit(solution)/shard_map/third/pallas_call | solution.py:129
  110.0 2.1 copy-done.1
  112.1 21.2 %second.2 = (f32[8,40,64,128]{3,2,1,0:T(8,128)}, f32[8,8,64,128]{3,2,1,0:T(8,128)S(1)}) custom-call(f32[2,64,128,512]{3,2,1,0:T(8,128)} %k_ref.11, f32[320,512]{1,0:T(8,128)S(1)} %bitcast.124, f32[64,512]{1,0:T(8,128)S(1)} %slice_bitcast_fusion.1.refs_1_), custom_call_target="tpu_custom_call" | custom-call | flops 9663676 | bytes 29360 | tf_op jit(solution)/shard_map/second/pallas_call | solution.py:88
  133.3 1.3 copy-done.3
  134.7 4.7 %all-to-all-done.t_ref = f32[8,16,64,128]{3,2,1,0:T(8,128)} async-done(((f32[8,16,64,128]{3,2,1,0:T(8,128)}), f32[8,16,64,128]{3,2,1,0:T(8,128)}, u32[]{:S(2)}, u32[]{:S(2)}) %all-to-all-start) | async-done | bytes 4194336 | tf_op jit(solution)/shard_map/all_to_all | solution.py:282
  139.4 5.3 %all-to-all-start.1 = ((f32[8,40,64,128]{3,2,1,0:T(8,128)}), f32[8,40,64,128]{3,2,1,0:T(8,128)}, u32[]{:S(2)}, u32[]{:S(2)}) async-start(f32[8,40,64,128]{3,2,1,0:T(8,128)} %get-tuple-element.32), calls=%async_computation.1 | async-start | bytes 20971520 | tf_op jit(solution)/shard_map/all_to_all | solution.py:282
  144.8 1.6 collective-permute-start.15
  148.4 3.8 collective-permute-done.14.refs_1_
  152.3 86.3 %collective-permute-done.15.refs_2_ = f32[64,128,128]{2,1,0:T(8,128)} collective-permute-done((f32[64,128,128]{2,1,0:T(8,128)}, f32[64,128,128]{2,1,0:T(8,128)}, u32[]{:S(2)}, u32[]{:S(2)}) %collective-permute-start.15) | collective-permute-done | bytes 4194336 | tf_op jit(solution)/shard_map/ppermute | solution.py:279
  238.5 89.0 %collective-permute-done.16.refs_3_ = f32[64,128,128]{2,1,0:T(8,128)} collective-permute-done((f32[64,128,128]{2,1,0:T(8,128)}, f32[64,128,128]{2,1,0:T(8,128)}, u32[]{:S(2)}, u32[]{:S(2)}) %collective-permute-start.16) | collective-permute-done | bytes 4194336 | tf_op jit(solution)/shard_map/ppermute | solution.py:279
  327.5 2.2 copy-done.2
  329.7 26.7 %first.1.q_ref = f32[64,512,128]{2,1,0:T(8,128)} custom-call(s32[4]{0:T(128)S(1)} %pad_add_fusion.off_ref, f32[2,64,128,512]{3,2,1,0:T(8,128)} %k_ref.11, f32[512,512]{1,0:T(8,128)S(1)} %get-tuple-element.42.d_ref, f32[64,128,128]{2,1,0:T(8,128)S(1)} %copy-done.2, f32[64,128,128]{2,1,0:T(8,128)} %collective-permute-done.14.refs_1_, ...), custom_call_target="tpu_custom_call" | custom-call | flops 12884901 | bytes 50331 | tf_op jit(solution)/shard_map/first/pallas_call | solution.py:174
  356.5 9.2 %finish.3 = (f32[64,128,512]{2,1,0:T(8,128)}, f32[4,512,128]{2,1,0:T(8,128)S(1)}) custom-call(f32[64]{0:T(128)S(1)} %dynamic-slice_subtract_fusion.eb_ref, f32[1,128]{1,0:T(1,128)S(1)} %dynamic-slice_bitcast_fusion.16.ec_ref, f32[512,128]{1,0:T(8,128)S(1)} %broadcast_in_dim.44.ea_ref, f32[2,64,128,512]{3,2,1,0:T(8,128)} %k_ref.11, ...), custom_call_target="tpu_custom_call" | custom-call | flops 3221225 | bytes 16777 | tf_op jit(solution)/shard_map/finish/pallas_call | solution.py:224
  365.7 1.0 copy-done.5
  366.7 4.8 %all-to-all-done.1.t_ref = f32[8,40,64,128]{3,2,1,0:T(8,128)} async-done(((f32[8,40,64,128]{3,2,1,0:T(8,128)}), f32[8,40,64,128]{3,2,1,0:T(8,128)}, u32[]{:S(2)}, u32[]{:S(2)}) %all-to-all-start.1) | async-done | bytes 10485792 | tf_op jit(solution)/shard_map/all_to_all | solution.py:282
  371.4 3.8 all-to-all-start.2
  375.3 1.2 copy-done.6
  376.5 20.1 %finish.4 = (f32[64,128,512]{2,1,0:T(8,128)}, f32[4,512,128]{2,1,0:T(8,128)S(1)}) custom-call(f32[64]{0:T(128)S(1)} %dynamic-slice_subtract_fusion.eb_ref, f32[1,128]{1,0:T(1,128)S(1)} %dynamic-slice_bitcast_fusion.16.ec_ref, f32[512,128]{1,0:T(8,128)S(1)} %broadcast_in_dim.44.ea_ref, f32[2,64,128,512]{3,2,1,0:T(8,128)} %k_ref.11, ...), custom_call_target="tpu_custom_call", output_to_operand_aliasing={{0}: (6, {})} | custom-call | flops 8053063 | bytes 41943 | tf_op jit(solution)/shard_map/finish/pallas_call | solution.py:224
  396.6 27.0 %all-to-all-done.2.t_ref = f32[8,8,64,128]{3,2,1,0:T(8,128)S(1)} async-done(((f32[8,8,64,128]{3,2,1,0:T(8,128)}), f32[8,8,64,128]{3,2,1,0:T(8,128)S(1)}, u32[]{:S(2)}, u32[]{:S(2)}) %all-to-all-start.2) | async-done | bytes 2097184 | tf_op jit(solution)/shard_map/all_to_all | solution.py:282
  423.5 5.2 %finish.5 = (f32[64,128,512]{2,1,0:T(8,128)}, f32[4,512,128]{2,1,0:T(8,128)S(1)}) custom-call(f32[64]{0:T(128)S(1)} %dynamic-slice_subtract_fusion.eb_ref, f32[1,128]{1,0:T(1,128)S(1)} %dynamic-slice_bitcast_fusion.16.ec_ref, f32[512,128]{1,0:T(8,128)S(1)} %broadcast_in_dim.44.ea_ref, f32[2,64,128,512]{3,2,1,0:T(8,128)} %k_ref.11, ...), custom_call_target="tpu_custom_call", output_to_operand_aliasing={{0}: (6, {})} | custom-call | flops 1610612 | bytes 8388 | tf_op jit(solution)/shard_map/finish/pallas_call | solution.py:224
  428.7 1.0 copy-done.4
  429.8 1.9 collective-permute-done.17
  431.7 1.1 bitcast_add_fusion
  432.8 1.6 collective-permute-start.18
  434.4 6.8 %collective-permute-done.18 = f32[1,512,128]{2,1,0:T(8,128)S(1)} collective-permute-done((f32[1,512,128]{2,1,0:T(8,128)S(1)}, f32[1,512,128]{2,1,0:T(8,128)S(1)}, u32[]{:S(2)}, u32[]{:S(2)}) %collective-permute-start.18) | collective-permute-done | bytes 262176 | tf_op jit(solution)/shard_map/ppermute | solution.py:279
  441.3 2.4 collective-permute-start.25
  443.7 2.4 collective-permute-start.24
  446.1 3.0 collective-permute-start.22
  449.0 2.9 collective-permute-start.20
  452.5 1.3 collective-permute-done.21
  454.2 1.7 collective-permute-done.19
  (87 shorter events, 9.7 us)
Async XLA Ops:
  1.4 8.8 %collective-permute-start = (f32[16,512]{1,0:T(8,128)S(1)}, f32[16,512]{1,0:T(8,128)S(1)}, u32[]{:S(2)}, u32[]{:S(2)}) collective-permute-start(f32[16,512]{1,0:T(8,128)S(1)} %get-tuple-element.53), channel_id=1, source_target_pairs={{0,4},{4,0},{8,12},{12,8},{16,20},{20,16},{24,28},{28,24},{1,5},{5... | collective-permute-start | bytes 98312 | tf_op jit(solution)/shard_map/ppermute | solution.py:276
  4.3 9.5 %collective-permute-start.1 = (f32[16,512]{1,0:T(8,128)S(1)}, f32[16,512]{1,0:T(8,128)S(1)}, u32[]{:S(2)}, u32[]{:S(2)}) collective-permute-start(f32[16,512]{1,0:T(8,128)S(1)} %get-tuple-element.53), channel_id=1, source_target_pairs={{0,8},{4,12},{8,0},{12,4},{16,24},{20,28},{24,16},{28,20},{1,9},{5... | collective-permute-start | bytes 98312 | tf_op jit(solution)/shard_map/ppermute | solution.py:276
  5.9 7.9 %collective-permute-start.2 = (f32[16,512]{1,0:T(8,128)S(1)}, f32[16,512]{1,0:T(8,128)S(1)}, u32[]{:S(2)}, u32[]{:S(2)}) collective-permute-start(f32[16,512]{1,0:T(8,128)S(1)} %get-tuple-element.53), channel_id=1, source_target_pairs={{0,12},{4,8},{8,4},{12,0},{16,28},{20,24},{24,20},{28,16},{1,13},{... | collective-permute-start | bytes 98312 | tf_op jit(solution)/shard_map/ppermute | solution.py:276
  5.9 8.0 %collective-permute-start.3 = (f32[16,512]{1,0:T(8,128)S(1)}, f32[16,512]{1,0:T(8,128)S(1)}, u32[]{:S(2)}, u32[]{:S(2)}) collective-permute-start(f32[16,512]{1,0:T(8,128)S(1)} %get-tuple-element.53), channel_id=1, source_target_pairs={{0,16},{4,20},{8,24},{12,28},{16,0},{20,4},{24,8},{28,12},{1,17},{... | collective-permute-start | bytes 98312 | tf_op jit(solution)/shard_map/ppermute | solution.py:276
  8.9 5.9 %collective-permute-start.4 = (f32[16,512]{1,0:T(8,128)S(1)}, f32[16,512]{1,0:T(8,128)S(1)}, u32[]{:S(2)}, u32[]{:S(2)}) collective-permute-start(f32[16,512]{1,0:T(8,128)S(1)} %get-tuple-element.53), channel_id=1, source_target_pairs={{0,20},{4,16},{8,28},{12,24},{16,4},{20,0},{24,12},{28,8},{1,21},{... | collective-permute-start | bytes 98312 | tf_op jit(solution)/shard_map/ppermute | solution.py:276
  10.2 5.8 %collective-permute-start.5 = (f32[16,512]{1,0:T(8,128)S(1)}, f32[16,512]{1,0:T(8,128)S(1)}, u32[]{:S(2)}, u32[]{:S(2)}) collective-permute-start(f32[16,512]{1,0:T(8,128)S(1)} %get-tuple-element.53), channel_id=1, source_target_pairs={{0,24},{4,28},{8,16},{12,20},{16,8},{20,12},{24,0},{28,4},{1,25},{... | collective-permute-start | bytes 98312 | tf_op jit(solution)/shard_map/ppermute | solution.py:276
  13.8 6.6 %collective-permute-start.6 = (f32[16,512]{1,0:T(8,128)S(1)}, f32[16,512]{1,0:T(8,128)S(1)}, u32[]{:S(2)}, u32[]{:S(2)}) collective-permute-start(f32[16,512]{1,0:T(8,128)S(1)} %get-tuple-element.53), channel_id=1, source_target_pairs={{0,28},{4,24},{8,20},{12,16},{16,12},{20,8},{24,4},{28,0},{1,29},{... | collective-permute-start | bytes 98312 | tf_op jit(solution)/shard_map/ppermute | solution.py:276
  21.5 6.6 %collective-permute-start.9 = (f32[3,64,128]{2,1,0:T(8,128)S(1)}, f32[3,64,128]{2,1,0:T(8,128)S(1)}, u32[]{:S(2)}, u32[]{:S(2)}) collective-permute-start(f32[3,64,128]{2,1,0:T(8,128)S(1)} %constant_dynamic-slice_fusion.1), channel_id=1, source_target_pairs={{0,24},{4,28},{8,16},{12,20},{16,8},{20,12},{24,0},{28,4},{1,25},{... | collective-permute-start | bytes 294920 | tf_op jit(solution)/shard_map/ppermute | solution.py:276
  21.7 7.8 %collective-permute-start.8 = (f32[3,64,128]{2,1,0:T(8,128)S(1)}, f32[3,64,128]{2,1,0:T(8,128)S(1)}, u32[]{:S(2)}, u32[]{:S(2)}) collective-permute-start(f32[3,64,128]{2,1,0:T(8,128)S(1)} %constant_dynamic-slice_fusion.1), channel_id=1, source_target_pairs={{0,16},{4,20},{8,24},{12,28},{16,0},{20,4},{24,8},{28,12},{1,17},{... | collective-permute-start | bytes 294920 | tf_op jit(solution)/shard_map/ppermute | solution.py:276
  21.7 7.8 %collective-permute-start.7 = (f32[3,64,128]{2,1,0:T(8,128)S(1)}, f32[3,64,128]{2,1,0:T(8,128)S(1)}, u32[]{:S(2)}, u32[]{:S(2)}) collective-permute-start(f32[3,64,128]{2,1,0:T(8,128)S(1)} %constant_dynamic-slice_fusion.1), channel_id=1, source_target_pairs={{0,8},{4,12},{8,0},{12,4},{16,24},{20,28},{24,16},{28,20},{1,9},{5... | collective-permute-start | bytes 294920 | tf_op jit(solution)/shard_map/ppermute | solution.py:276
  29.6 15.2 %collective-permute-start.10 = (f32[4,3,64,128]{3,2,1,0:T(8,128)S(1)}, f32[4,3,64,128]{3,2,1,0:T(8,128)S(1)}, u32[]{:S(2)}, u32[]{:S(2)}) collective-permute-start(f32[4,3,64,128]{3,2,1,0:T(8,128)S(1)} %get-tuple-element.52), channel_id=1, source_target_pairs={{0,4},{4,0},{8,12},{12,8},{16,20},{20,16},{24,28},{28,24},{1,5},{5... | collective-permute-start | bytes 1179656 | tf_op jit(solution)/shard_map/ppermute | solution.py:276
  42.8 1.9 copy-start
  45.0 94.4 %all-to-all-start = ((f32[8,16,64,128]{3,2,1,0:T(8,128)}), f32[8,16,64,128]{3,2,1,0:T(8,128)}, u32[]{:S(2)}, u32[]{:S(2)}) async-start(f32[8,16,64,128]{3,2,1,0:T(8,128)} %copy-done), calls=%async_computation | async-start | bytes 8388608 | tf_op jit(solution)/shard_map/all_to_all | solution.py:282
  49.6 19.8 %collective-permute-start.13 = (f32[3,512,128]{2,1,0:T(8,128)S(1)}, f32[3,512,128]{2,1,0:T(8,128)S(1)}, u32[]{:S(2)}, u32[]{:S(2)}) collective-permute-start(f32[3,512,128]{2,1,0:T(8,128)S(1)} %bitcast_dynamic-update-slice_fusion), channel_id=1, source_target_pairs={{0,3},{1,2},{2,1},{3,0},{4,7},{5,6},{6,5},{7,4},{8,11},{9,10},{10,... | collective-permute-start | bytes 2359304 | tf_op jit(solution)/shard_map/ppermute | solution.py:279
  49.7 36.7 %collective-permute-start.12 = (f32[3,512,128]{2,1,0:T(8,128)S(1)}, f32[3,512,128]{2,1,0:T(8,128)S(1)}, u32[]{:S(2)}, u32[]{:S(2)}) collective-permute-start(f32[3,512,128]{2,1,0:T(8,128)S(1)} %bitcast_dynamic-update-slice_fusion), channel_id=1, source_target_pairs={{0,2},{1,3},{2,0},{3,1},{4,6},{5,7},{6,4},{7,5},{8,10},{9,11},{10,... | collective-permute-start | bytes 2359304 | tf_op jit(solution)/shard_map/ppermute | solution.py:279
  51.3 35.1 %collective-permute-start.11 = (f32[3,512,128]{2,1,0:T(8,128)S(1)}, f32[3,512,128]{2,1,0:T(8,128)S(1)}, u32[]{:S(2)}, u32[]{:S(2)}) collective-permute-start(f32[3,512,128]{2,1,0:T(8,128)S(1)} %bitcast_dynamic-update-slice_fusion), channel_id=1, source_target_pairs={{0,1},{1,0},{2,3},{3,2},{4,5},{5,4},{6,7},{7,6},{8,9},{9,8},{10,11... | collective-permute-start | bytes 2359304 | tf_op jit(solution)/shard_map/ppermute | solution.py:279
  110.0 2.1 copy-start.1
  133.3 1.3 copy-start.3
  139.4 7.3 %copy-start.7 = (f32[512]{0:T(512)S(1)}, f32[512]{0:T(512)}, u32[]{:S(2)}) copy-start(f32[512]{0:T(512)} %param.9) | copy-start | bytes 6148
  139.4 7.3 %copy-start.8 = (s32[512]{0:T(512)S(1)}, s32[512]{0:T(512)}, u32[]{:S(2)}) copy-start(s32[512]{0:T(512)} %param.11) | copy-start | bytes 6148
  139.4 7.6 %copy-start.9 = (f32[100]{0:T(128)S(1)}, f32[100]{0:T(128)}, u32[]{:S(2)}) copy-start(f32[100]{0:T(128)} %param.8) | copy-start | bytes 1204
  139.4 7.6 %copy-start.10 = (s32[3]{0:T(128)S(1)}, s32[3]{0:T(128)}, u32[]{:S(2)}) copy-start(s32[3]{0:T(128)} %param.10) | copy-start | bytes 40
  139.4 232.1 %all-to-all-start.1 = ((f32[8,40,64,128]{3,2,1,0:T(8,128)}), f32[8,40,64,128]{3,2,1,0:T(8,128)}, u32[]{:S(2)}, u32[]{:S(2)}) async-start(f32[8,40,64,128]{3,2,1,0:T(8,128)} %get-tuple-element.32), calls=%async_computation.1 | async-start | bytes 20971520 | tf_op jit(solution)/shard_map/all_to_all | solution.py:282
  144.7 7.6 %collective-permute-start.14 = (f32[64,128,128]{2,1,0:T(8,128)}, f32[64,128,128]{2,1,0:T(8,128)}, u32[]{:S(2)}, u32[]{:S(2)}) collective-permute-start(f32[64,128,128]{2,1,0:T(8,128)} %get-tuple-element.23), channel_id=1, source_target_pairs={{0,1},{1,0},{2,3},{3,2},{4,5},{5,4},{6,7},{7,6},{8,9},{9,8},{10,11... | collective-permute-start | bytes 12582920 | tf_op jit(solution)/shard_map/ppermute | solution.py:279
  144.8 93.8 %collective-permute-start.15 = (f32[64,128,128]{2,1,0:T(8,128)}, f32[64,128,128]{2,1,0:T(8,128)}, u32[]{:S(2)}, u32[]{:S(2)}) collective-permute-start(f32[64,128,128]{2,1,0:T(8,128)} %get-tuple-element.24), channel_id=1, source_target_pairs={{0,2},{1,3},{2,0},{3,1},{4,6},{5,7},{6,4},{7,5},{8,10},{9,11},{10,... | collective-permute-start | bytes 12582920 | tf_op jit(solution)/shard_map/ppermute | solution.py:279
  146.4 181.1 %collective-permute-start.16 = (f32[64,128,128]{2,1,0:T(8,128)}, f32[64,128,128]{2,1,0:T(8,128)}, u32[]{:S(2)}, u32[]{:S(2)}) collective-permute-start(f32[64,128,128]{2,1,0:T(8,128)} %get-tuple-element.25), channel_id=1, source_target_pairs={{0,3},{1,2},{2,1},{3,0},{4,7},{5,6},{6,5},{7,4},{8,11},{9,10},{10,... | collective-permute-start | bytes 12582920 | tf_op jit(solution)/shard_map/ppermute | solution.py:279
  327.5 2.2 copy-start.2
  365.7 1.0 copy-start.5
  371.4 52.1 %all-to-all-start.2 = ((f32[8,8,64,128]{3,2,1,0:T(8,128)}), f32[8,8,64,128]{3,2,1,0:T(8,128)S(1)}, u32[]{:S(2)}, u32[]{:S(2)}) async-start(f32[8,8,64,128]{3,2,1,0:T(8,128)} %copy-done.3), calls=%async_computation.2 | async-start | bytes 4194304 | tf_op jit(solution)/shard_map/all_to_all | solution.py:282
  375.3 1.2 copy-start.6
  428.7 1.0 copy-start.4
  429.7 2.0 collective-permute-start.17
  432.8 8.4 %collective-permute-start.18 = (f32[1,512,128]{2,1,0:T(8,128)S(1)}, f32[1,512,128]{2,1,0:T(8,128)S(1)}, u32[]{:S(2)}, u32[]{:S(2)}) collective-permute-start(f32[1,512,128]{2,1,0:T(8,128)S(1)} %constant_dynamic-slice_fusion), channel_id=1, source_target_pairs={{0,2},{1,3},{2,0},{3,1},{4,6},{5,7},{6,4},{7,5},{8,10},{9,11},{10,... | collective-permute-start | bytes 786440 | tf_op jit(solution)/shard_map/ppermute | solution.py:279
  441.3 7.7 %collective-permute-start.25 = (f32[64,128]{1,0:T(8,128)S(1)}, f32[64,128]{1,0:T(8,128)S(1)}, u32[]{:S(2)}, u32[]{:S(2)}) collective-permute-start(f32[64,128]{1,0:T(8,128)S(1)} %get-tuple-element.56), channel_id=1, source_target_pairs={{0,28},{4,24},{8,20},{12,16},{16,12},{20,8},{24,4},{28,0},{1,29},{... | collective-permute-start | bytes 98312 | tf_op jit(solution)/shard_map/ppermute | solution.py:276
  443.7 8.2 %collective-permute-start.24 = (f32[64,128]{1,0:T(8,128)S(1)}, f32[64,128]{1,0:T(8,128)S(1)}, u32[]{:S(2)}, u32[]{:S(2)}) collective-permute-start(f32[64,128]{1,0:T(8,128)S(1)} %get-tuple-element.57), channel_id=1, source_target_pairs={{0,24},{4,28},{8,16},{12,20},{16,8},{20,12},{24,0},{28,4},{1,25},{... | collective-permute-start | bytes 98312 | tf_op jit(solution)/shard_map/ppermute | solution.py:276
  446.1 6.5 %collective-permute-start.23 = (f32[64,128]{1,0:T(8,128)S(1)}, f32[64,128]{1,0:T(8,128)S(1)}, u32[]{:S(2)}, u32[]{:S(2)}) collective-permute-start(f32[64,128]{1,0:T(8,128)S(1)} %get-tuple-element.58), channel_id=1, source_target_pairs={{0,20},{4,16},{8,28},{12,24},{16,4},{20,0},{24,12},{28,8},{1,21},{... | collective-permute-start | bytes 98312 | tf_op jit(solution)/shard_map/ppermute | solution.py:276
  446.1 6.5 %collective-permute-start.22 = (f32[64,128]{1,0:T(8,128)S(1)}, f32[64,128]{1,0:T(8,128)S(1)}, u32[]{:S(2)}, u32[]{:S(2)}) collective-permute-start(f32[64,128]{1,0:T(8,128)S(1)} %get-tuple-element.59), channel_id=1, source_target_pairs={{0,16},{4,20},{8,24},{12,28},{16,0},{20,4},{24,8},{28,12},{1,17},{... | collective-permute-start | bytes 98312 | tf_op jit(solution)/shard_map/ppermute | solution.py:276
  449.0 4.8 %collective-permute-start.21 = (f32[64,128]{1,0:T(8,128)S(1)}, f32[64,128]{1,0:T(8,128)S(1)}, u32[]{:S(2)}, u32[]{:S(2)}) collective-permute-start(f32[64,128]{1,0:T(8,128)S(1)} %get-tuple-element.60), channel_id=1, source_target_pairs={{0,12},{4,8},{8,4},{12,0},{16,28},{20,24},{24,20},{28,16},{1,13},{... | collective-permute-start | bytes 98312 | tf_op jit(solution)/shard_map/ppermute | solution.py:276
  449.0 5.1 %collective-permute-start.20 = (f32[64,128]{1,0:T(8,128)S(1)}, f32[64,128]{1,0:T(8,128)S(1)}, u32[]{:S(2)}, u32[]{:S(2)}) collective-permute-start(f32[64,128]{1,0:T(8,128)S(1)} %get-tuple-element.61), channel_id=1, source_target_pairs={{0,8},{4,12},{8,0},{12,4},{16,24},{20,28},{24,16},{28,20},{1,9},{5... | collective-permute-start | bytes 98312 | tf_op jit(solution)/shard_map/ppermute | solution.py:276
  451.9 3.9 collective-permute-start.19

commit v2 on v1

--- a/solution.py
+++ b/solution.py
@@ -93,7 +93,7 @@
         out_specs=[
             pl.BlockSpec((peers, h // peers, tile, nc), lambda s: (0, 0, s, 0)) for h in heights
         ],
-        out_shape=[jax.ShapeDtypeStruct((peers, h // peers, na, nc), F32) for h in heights],
+        out_shape=[pltpu.HBM((peers, h // peers, na, nc), F32) for h in heights],
         scratch_shapes=[
             pltpu.VMEM((tile * width, nc), F32),
             pltpu.VMEM((2 * width, depth), BF16),
@@ -134,7 +134,7 @@
             pl.BlockSpec((total, depth), lambda s: (0, 0)),
         ],
         out_specs=[pl.BlockSpec((tile, na, nc), lambda s: (s, 0, 0))] * blocks,
-        out_shape=[jax.ShapeDtypeStruct((nb, na, nc), F32)] * blocks,
+        out_shape=[pltpu.HBM((nb, na, nc), F32)] * blocks,
         scratch_shapes=[pltpu.VMEM((depth, total), BF16)] * 2,
         name="third",
         **params(flops, size),
@@ -184,7 +184,7 @@
             out_specs=pl.BlockSpec((tile, total, nc), lambda s, o: (s, 0, 0)),
             scratch_shapes=[pltpu.VMEM((2 * total, depth), BF16)],
         ),
-        out_shape=jax.ShapeDtypeStruct((nb, total, nc), F32),
+        out_shape=pltpu.HBM((nb, total, nc), F32),
         name="first",
         **params(flops, size),
     )(offsets, integrals, d_rows, *thirds)
@@ -243,8 +243,8 @@
             ],
         ),
         out_shape=[
-            jax.ShapeDtypeStruct((base.shape[0], nc, total), F32),
-            jax.ShapeDtypeStruct((depth // nc, total, nc), F32),
+            pltpu.HBM((base.shape[0], nc, total), F32),
+            pltpu.HBM((depth // nc, total, nc), F32),
         ],
         input_output_aliases={6: 0} if given else {},
         name="finish",
@@ -288,20 +288,36 @@
         ]
         return jnp.concatenate(ordered, axis=axis)
 
-    lots = [nb // 4, nb - nb // 4 - nb // 8, nb // 8]
+    few = max(nb // 16, 4)
+    lots = [nb // 4, nb - nb // 4 - few, few]
     starts = [0, lots[0], lots[0] + lots[1]]
 
+    share = depth // m
     own = doubles[1][: lots[0]]
-    rows = in_order([over_b(own, k) for k in range(n)], i, 0)
+    own = jnp.concatenate([own[:, q * share : (q + 1) * share] for q in range(m)])
+    part = lax.dynamic_slice_in_dim(doubles, j * share, share, axis=2)
+    head = jnp.concatenate([own, part.reshape(3 * nb, share)])
+    head = jnp.stack([over_b(head, k) for k in range(0, n, 2)])
+
+    def from_last_bit(x):
+        x = jnp.stack([x, over_b(x, 1)], axis=1)
+        x = x.reshape((n,) + x.shape[2:])
+        return jnp.stack([lax.dynamic_index_in_dim(x, i ^ p, 0, False) for p in range(n)])
+
+    rows = from_last_bit(head[:, : m * lots[0]]).reshape(n, m, lots[0], share)
+    rows = jnp.concatenate([rows[:, q] for q in range(m)], axis=2).reshape(n * lots[0], depth)
+    part = from_last_bit(tie(head[:, m * lots[0] :], rows))
     (lot,) = second(integrals, (rows,), n)
-
-    share = depth // m
-    part = lax.dynamic_slice_in_dim(tie(doubles, rows), j * share, share, axis=2)
-    part = jnp.stack([over_b(part, k) for k in range(0, n, 2)])
-    part = jnp.stack([part, over_b(part, 1)], axis=1).reshape((n,) + part.shape[1:])
-    part = in_order([part[k] for k in range(n)], i, 1)
-    arrived = [all_over_b(tie(lot, part))]
-    full = in_order([over_c(part, q) for q in range(m)], j, 2)
+    part, lot = lax.optimization_barrier((part, lot))
+    arrived = [all_over_b(lot)]
+
+    part = part.reshape(n, 3, nb, share).transpose(1, 0, 2, 3).reshape(3, total, share)
+    step, bits = m // 2, 0
+    while step:
+        part = jnp.stack([part, over_c(part, step)], axis=bits)
+        step, bits = step // 2, bits + 1
+    part = part.reshape((m,) + part.shape[bits:])
+    full = in_order([part[q] for q in range(m)], j, 2)
 
     d2 = jnp.concatenate([lax.dynamic_slice_in_dim(full[2], (j ^ q) * nc, nc) for q in range(m)])
     thirds = third(integrals, d2, m)
@@ -339,9 +355,7 @@
         step *= 2
     grad = grad.reshape(total, nc)
 
-    grad = sum(
-        over_b(lax.dynamic_slice_in_dim(grad, (i ^ k) * nb, nb), k) for k in range(n)
-    )
+    grad = jnp.sum(all_over_b(grad.reshape(n, nb, nc)), axis=0)
     return amplitudes, grad
 
 

time: 458 us -> 453 us (0.989)
  starting transfers between devices: 48.1 us -> 28.2 us
  blocking collectives: 0 us -> 12.6 us
  Pallas kernels: 117 us -> 122 us
    ppermute x18 -> x5, starting transfers between devices: 28.9 us -> 8.87 us  [over_b(): return lax.ppermute(x, 'vb', [(p, p ^ k) for p in range(n)]) if k else x]
    ppermute x8 -> x7, waiting for transfers between devices: 223 us -> 207 us  [over_c(): return lax.ppermute(x, 'vc', [(p, p ^ k) for p in range(m)]) if k else x]
    all_to_all x3, waiting for transfers between devices: 36.4 us -> 50.2 us  [all_over_b(): return lax.all_to_all(x, 'vb', split_axis=0, concat_axis=0, tiled=True)]
    all_to_all x0 -> x1, blocking collectives: none -> 12.6 us  [all_over_b(): return lax.all_to_all(x, 'vb', split_axis=0, concat_axis=0, tiled=True)]
    unnamed x42 -> x32, local copies, waits for them, and re-layouts: 10.9 us -> 4.86 us
    ppermute x18 -> x5, waiting for transfers between devices: 12.6 us -> 13.8 us  [over_b(): return lax.ppermute(x, 'vb', [(p, p ^ k) for p in range(n)]) if k else x]
  transfers between devices with their start and end apart: 29 -> 15, of which waited for: 18 -> 13; matrix products, arithmetic and copies ran while one was open for 1% -> 2% of each run, Pallas kernels for 25% -> 26%
where the time goes in v2:
time: 453 us; the launch traced here: 451 us
  waiting for transfers between devices  271 us (60%)
  Pallas kernels  122 us (27%)
  starting transfers between devices  28.2 us (6%)
  blocking collectives  12.6 us (3%)
  local copies, waits for them, and re-layouts  11.1 us (2%)
  other arithmetic  5.78 us (1%)
    ppermute x7, waiting for transfers between devices, over_c(): return lax.ppermute(x, 'vc', [(p, p ^ k) for p in range(m)]) if k else x  207 us
    all_to_all x3, waiting for transfers between devices, all_over_b(): return lax.all_to_all(x, 'vb', split_axis=0, concat_axis=0, tiled=True)  50.2 us
    pallas_call x3, Pallas kernels, finish(): pl.pallas_call(functools.partial(finish_kernel, b0), grid_spec=pltpu.Pref...  37 us
    pallas_call x2, Pallas kernels, second(): pl.pallas_call(functools.partial(second_kernel, peers, tile, per_dot), gr...  34.9 us
    pallas_call x1, Pallas kernels, first(): pl.pallas_call(functools.partial(first_kernel, per_dot), grid_spec=pltpu....  26.7 us
    pallas_call x1, Pallas kernels, third(): pl.pallas_call(third_kernel, grid=(nb // tile,), in_specs=[pl.BlockSpec((...  23.2 us
    all_to_all x3, starting transfers between devices, all_over_b(): return lax.all_to_all(x, 'vb', split_axis=0, concat_axis=0, tiled=True)  14 us
    ppermute x5, waiting for transfers between devices, over_b(): return lax.ppermute(x, 'vb', [(p, p ^ k) for p in range(n)]) if k else x  13.8 us
  transfers between devices with their start and end apart: 15, of which 13 were waited for; matrix products, arithmetic and copies ran while one was open for 2% of the time, Pallas kernels for 26%

profile of v2, /device:TPU:0, one launch (start us, length us, event | category | flops | bytes accessed | tf_op | source)
XLA Modules:
  0.0 451.4 jit_solution(5917264412059851636)
XLA Ops:
  0.6 0.8 slice_bitcast_fusion.1
  1.4 0.9 constant_dynamic-slice_fusion.1
  2.3 5.1 %collective-permute-start.2 = (f32[256,128]{1,0:T(8,128)S(1)}, f32[256,128]{1,0:T(8,128)S(1)}, u32[]{:S(2)}, u32[]{:S(2)}) collective-permute-start(f32[256,128]{1,0:T(8,128)S(1)} %constant_dynamic-update-slice_fusion), channel_id=1, source_target_pairs={{0,24},{4,28},{8,16},{12,20},{16,8},{20,12},{24,0},{28,4},{1,25},{... | collective-permute-start | bytes 393224 | tf_op jit(solution)/shard_map/ppermute | solution.py:276
  7.5 0.6 collective-permute-start
  8.1 3.8 collective-permute-done.2
  11.9 6.6 %collective-permute-done.1 = f32[256,128]{1,0:T(8,128)S(1)} collective-permute-done((f32[256,128]{1,0:T(8,128)S(1)}, f32[256,128]{1,0:T(8,128)S(1)}, u32[]{:S(2)}, u32[]{:S(2)}) %collective-permute-start.1) | collective-permute-done | bytes 131104 | tf_op jit(solution)/shard_map/ppermute | solution.py:276
  18.5 1.6 collective-permute-start.3
  20.2 3.4 collective-permute-done.3
  23.8 1.6 collective-permute-start.4
  25.4 13.7 %second.2 = f32[8,16,64,128]{3,2,1,0:T(8,128)} custom-call(f32[2,64,128,512]{3,2,1,0:T(8,128)} %k_ref.11, f32[128,512]{1,0:T(8,128)S(1)} %pad_maximum_fusion.7.refs_0_), custom_call_target="tpu_custom_call" | custom-call | flops 3221225 | bytes 20971 | tf_op jit(solution)/shard_map/second/pallas_call | solution.py:88
  39.4 4.6 %all-to-all-start = ((f32[8,16,64,128]{3,2,1,0:T(8,128)}), f32[8,16,64,128]{3,2,1,0:T(8,128)}, u32[]{:S(2)}, u32[]{:S(2)}) async-start(f32[8,16,64,128]{3,2,1,0:T(8,128)} %second.2), calls=%async_computation | async-start | bytes 8388608 | tf_op jit(solution)/shard_map/all_to_all | solution.py:282
  44.0 1.6 collective-permute-start.5
  45.6 15.6 %collective-permute-done.5 = f32[3,512,128]{2,1,0:T(8,128)S(1)} collective-permute-done((f32[3,512,128]{2,1,0:T(8,128)S(1)}, f32[3,512,128]{2,1,0:T(8,128)S(1)}, u32[]{:S(2)}, u32[]{:S(2)}) %collective-permute-start.5) | collective-permute-done | bytes 786464 | tf_op jit(solution)/shard_map/ppermute | solution.py:279
  61.2 0.3 fusion
  61.6 3.5 collective-permute-done.6
  65.1 1.6 pad_maximum_fusion
  67.4 0.3 fusion.1
  67.7 0.9 slice.90
  68.7 1.2 reshape.65.refs_0_
  70.1 23.2 %third.1 = (f32[64,128,128]{2,1,0:T(8,128)}, f32[64,128,128]{2,1,0:T(8,128)}, f32[64,128,128]{2,1,0:T(8,128)}, f32[64,128,128]{2,1,0:T(8,128)}) custom-call(f32[2,64,128,512]{3,2,1,0:T(8,128)} %k_ref.11, f32[512,512]{1,0:T(8,128)S(1)} %pad_maximum_fusion.3.d_ref), custom_call_target="tpu_custom_call" | custom-call | flops 12884901 | bytes 33554 | tf_op jit(solution)/shard_map/third/pallas_call | solution.py:129
  93.3 21.2 %second.3 = (f32[8,44,64,128]{3,2,1,0:T(8,128)}, f32[8,4,64,128]{3,2,1,0:T(8,128)}) custom-call(f32[2,64,128,512]{3,2,1,0:T(8,128)} %k_ref.11, f32[352,512]{1,0:T(8,128)S(1)} %reshape.65.refs_0_, f32[32,512]{1,0:T(8,128)S(1)} %reshape.66.refs_1_), custom_call_target="tpu_custom_call" | custom-call | flops 9663676 | bytes 29360 | tf_op jit(solution)/shard_map/second/pallas_call | solution.py:88
  114.5 20.8 %all-to-all-done.t_ref = f32[8,16,64,128]{3,2,1,0:T(8,128)} async-done(((f32[8,16,64,128]{3,2,1,0:T(8,128)}), f32[8,16,64,128]{3,2,1,0:T(8,128)}, u32[]{:S(2)}, u32[]{:S(2)}) %all-to-all-start) | async-done | bytes 4194336 | tf_op jit(solution)/shard_map/all_to_all | solution.py:282
  135.3 5.4 %all-to-all-start.1 = ((f32[8,44,64,128]{3,2,1,0:T(8,128)}), f32[8,44,64,128]{3,2,1,0:T(8,128)}, u32[]{:S(2)}, u32[]{:S(2)}) async-start(f32[8,44,64,128]{3,2,1,0:T(8,128)} %get-tuple-element.34), calls=%async_computation.1 | async-start | bytes 23068672 | tf_op jit(solution)/shard_map/all_to_all | solution.py:282
  140.7 1.6 collective-permute-start.8
  142.3 0.3 collective-permute-start.9
  142.6 0.2 select_reduce_fusion
  142.9 0.7 select_reduce_fusion.1
  143.6 0.7 dynamic-slice_subtract_fusion.eb_ref
  144.4 3.8 collective-permute-done.7.refs_1_
  148.2 86.3 %collective-permute-done.8.refs_2_ = f32[64,128,128]{2,1,0:T(8,128)} collective-permute-done((f32[64,128,128]{2,1,0:T(8,128)}, f32[64,128,128]{2,1,0:T(8,128)}, u32[]{:S(2)}, u32[]{:S(2)}) %collective-permute-start.8) | collective-permute-done | bytes 4194336 | tf_op jit(solution)/shard_map/ppermute | solution.py:279
  234.5 89.0 %collective-permute-done.9.refs_3_ = f32[64,128,128]{2,1,0:T(8,128)} collective-permute-done((f32[64,128,128]{2,1,0:T(8,128)}, f32[64,128,128]{2,1,0:T(8,128)}, u32[]{:S(2)}, u32[]{:S(2)}) %collective-permute-start.9) | collective-permute-done | bytes 4194336 | tf_op jit(solution)/shard_map/ppermute | solution.py:279
  323.5 2.2 copy-done
  325.7 26.7 %first.1.q_ref = f32[64,512,128]{2,1,0:T(8,128)} custom-call(s32[4]{0:T(128)S(1)} %pad_add_fusion.off_ref, f32[2,64,128,512]{3,2,1,0:T(8,128)} %k_ref.11, f32[512,512]{1,0:T(8,128)S(1)} %get-tuple-element.44.d_ref, f32[64,128,128]{2,1,0:T(8,128)S(1)} %copy-done, f32[64,128,128]{2,1,0:T(8,128)} %collective-permute-done.7.refs_1_, ...), custom_call_target="tpu_custom_call" | custom-call | flops 12884901 | bytes 50331 | tf_op jit(solution)/shard_map/first/pallas_call | solution.py:174
  352.5 9.5 %finish.3 = (f32[64,128,512]{2,1,0:T(8,128)}, f32[4,512,128]{2,1,0:T(8,128)}) custom-call(f32[64]{0:T(128)S(1)} %dynamic-slice_subtract_fusion.eb_ref, f32[1,128]{1,0:T(1,128)S(1)} %dynamic-slice_bitcast_fusion.9.ec_ref, f32[512,128]{1,0:T(8,128)S(1)} %broadcast_in_dim.44.ea_ref, f32[2,64,128,512]{3,2,1,0:T(8,128)} %k_ref.11, f32[64,512,128]{2,1,0:T(8,128)} %first.1.q_ref, ...), custom_call_target="tpu_custom_call" | custom-call | flops 3221225 | bytes 16777 | tf_op jit(solution)/shard_map/finish/pallas_call | solution.py:224
  362.0 27.8 %all-to-all-done.1.t_ref = f32[8,44,64,128]{3,2,1,0:T(8,128)} async-done(((f32[8,44,64,128]{3,2,1,0:T(8,128)}), f32[8,44,64,128]{3,2,1,0:T(8,128)}, u32[]{:S(2)}, u32[]{:S(2)}) %all-to-all-start.1) | async-done | bytes 11534368 | tf_op jit(solution)/shard_map/all_to_all | solution.py:282
  389.8 4.1 all-to-all-start.2
  393.9 1.2 copy-done.1
  395.1 23.0 %finish.4 = (f32[64,128,512]{2,1,0:T(8,128)}, f32[4,512,128]{2,1,0:T(8,128)}) custom-call(f32[64]{0:T(128)S(1)} %dynamic-slice_subtract_fusion.eb_ref, f32[1,128]{1,0:T(1,128)S(1)} %dynamic-slice_bitcast_fusion.9.ec_ref, f32[512,128]{1,0:T(8,128)S(1)} %broadcast_in_dim.44.ea_ref, f32[2,64,128,512]{3,2,1,0:T(8,128)} %k_ref.11, ...), custom_call_target="tpu_custom_call", output_to_operand_aliasing={{0}: (6, {})} | custom-call | flops 8858370 | bytes 46137 | tf_op jit(solution)/shard_map/finish/pallas_call | solution.py:224
  418.1 1.7 all-to-all-done.2.t_ref
  419.8 1.2 copy-done.2
  421.1 4.5 finish.5
  425.5 1.1 dynamic-slice_bitcast_fusion.4
  426.7 1.9 collective-permute-done.10
  428.6 1.1 bitcast_add_fusion
  429.7 1.6 collective-permute-start.11
  431.3 6.8 %collective-permute-done.11 = f32[1,512,128]{2,1,0:T(8,128)S(1)} collective-permute-done((f32[1,512,128]{2,1,0:T(8,128)S(1)}, f32[1,512,128]{2,1,0:T(8,128)S(1)}, u32[]{:S(2)}, u32[]{:S(2)}) %collective-permute-start.11) | collective-permute-done | bytes 262176 | tf_op jit(solution)/shard_map/ppermute | solution.py:279
  438.1 12.6 %all_to_all.20 = f32[8,64,128]{2,1,0:T(8,128)S(1)} all-to-all(f32[8,64,128]{2,1,0:T(8,128)S(1)} %bitcast.98), channel_id=1, replica_groups=mesh['vb'=8,'vc'=4] {'vb'}, dimensions={0} | all-to-all | bytes 524288 | tf_op jit(solution)/shard_map/all_to_all | solution.py:282
  450.8 0.6 reduce_sum.29
  (60 shorter events, 2.0 us)
Async XLA Ops:
  2.3 9.5 %collective-permute-start.2 = (f32[256,128]{1,0:T(8,128)S(1)}, f32[256,128]{1,0:T(8,128)S(1)}, u32[]{:S(2)}, u32[]{:S(2)}) collective-permute-start(f32[256,128]{1,0:T(8,128)S(1)} %constant_dynamic-update-slice_fusion), channel_id=1, source_target_pairs={{0,24},{4,28},{8,16},{12,20},{16,8},{20,12},{24,0},{28,4},{1,25},{... | collective-permute-start | bytes 393224 | tf_op jit(solution)/shard_map/ppermute | solution.py:276
  7.5 11.1 %collective-permute-start.1 = (f32[256,128]{1,0:T(8,128)S(1)}, f32[256,128]{1,0:T(8,128)S(1)}, u32[]{:S(2)}, u32[]{:S(2)}) collective-permute-start(f32[256,128]{1,0:T(8,128)S(1)} %constant_dynamic-update-slice_fusion), channel_id=1, source_target_pairs={{0,16},{4,20},{8,24},{12,28},{16,0},{20,4},{24,8},{28,12},{1,17},{... | collective-permute-start | bytes 393224 | tf_op jit(solution)/shard_map/ppermute | solution.py:276
  7.5 11.1 %collective-permute-start = (f32[256,128]{1,0:T(8,128)S(1)}, f32[256,128]{1,0:T(8,128)S(1)}, u32[]{:S(2)}, u32[]{:S(2)}) collective-permute-start(f32[256,128]{1,0:T(8,128)S(1)} %constant_dynamic-update-slice_fusion), channel_id=1, source_target_pairs={{0,8},{4,12},{8,0},{12,4},{16,24},{20,28},{24,16},{28,20},{1,9},{5... | collective-permute-start | bytes 393224 | tf_op jit(solution)/shard_map/ppermute | solution.py:276
  18.5 5.0 %collective-permute-start.3 = (f32[4,64,128]{2,1,0:T(8,128)S(1)}, f32[4,64,128]{2,1,0:T(8,128)S(1)}, u32[]{:S(2)}, u32[]{:S(2)}) collective-permute-start(f32[4,64,128]{2,1,0:T(8,128)S(1)} %pad_maximum_fusion.8), channel_id=1, source_target_pairs={{0,4},{4,0},{8,12},{12,8},{16,20},{20,16},{24,28},{28,24},{1,5},{5... | collective-permute-start | bytes 393224 | tf_op jit(solution)/shard_map/ppermute | solution.py:276
  23.8 15.2 %collective-permute-start.4 = (f32[4,192,128]{2,1,0:T(8,128)S(1)}, f32[4,192,128]{2,1,0:T(8,128)S(1)}, u32[]{:S(2)}, u32[]{:S(2)}) collective-permute-start(f32[4,192,128]{2,1,0:T(8,128)S(1)} %slice.82), channel_id=1, source_target_pairs={{0,4},{4,0},{8,12},{12,8},{16,20},{20,16},{24,28},{28,24},{1,5},{5... | collective-permute-start | bytes 1179656 | tf_op jit(solution)/shard_map/ppermute | solution.py:276
  39.4 95.9 %all-to-all-start = ((f32[8,16,64,128]{3,2,1,0:T(8,128)}), f32[8,16,64,128]{3,2,1,0:T(8,128)}, u32[]{:S(2)}, u32[]{:S(2)}) async-start(f32[8,16,64,128]{3,2,1,0:T(8,128)} %second.2), calls=%async_computation | async-start | bytes 8388608 | tf_op jit(solution)/shard_map/all_to_all | solution.py:282
  44.0 17.2 %collective-permute-start.5 = (f32[3,512,128]{2,1,0:T(8,128)S(1)}, f32[3,512,128]{2,1,0:T(8,128)S(1)}, u32[]{:S(2)}, u32[]{:S(2)}) collective-permute-start(f32[3,512,128]{2,1,0:T(8,128)S(1)} %bitcast.73), channel_id=1, source_target_pairs={{0,2},{1,3},{2,0},{3,1},{4,6},{5,7},{6,4},{7,5},{8,10},{9,11},{10,... | collective-permute-start | bytes 2359304 | tf_op jit(solution)/shard_map/ppermute | solution.py:279
  61.5 3.6 collective-permute-start.6
  135.3 7.3 %copy-start.3 = (f32[512]{0:T(512)S(1)}, f32[512]{0:T(512)}, u32[]{:S(2)}) copy-start(f32[512]{0:T(512)} %param.9) | copy-start | bytes 6148
  135.3 7.3 %copy-start.4 = (s32[512]{0:T(512)S(1)}, s32[512]{0:T(512)}, u32[]{:S(2)}) copy-start(s32[512]{0:T(512)} %param.11) | copy-start | bytes 6148
  135.3 7.7 %copy-start.5 = (f32[100]{0:T(128)S(1)}, f32[100]{0:T(128)}, u32[]{:S(2)}) copy-start(f32[100]{0:T(128)} %param.8) | copy-start | bytes 1204
  135.3 7.7 %copy-start.6 = (s32[3]{0:T(128)S(1)}, s32[3]{0:T(128)}, u32[]{:S(2)}) copy-start(s32[3]{0:T(128)} %param.10) | copy-start | bytes 40
  135.3 254.5 %all-to-all-start.1 = ((f32[8,44,64,128]{3,2,1,0:T(8,128)}), f32[8,44,64,128]{3,2,1,0:T(8,128)}, u32[]{:S(2)}, u32[]{:S(2)}) async-start(f32[8,44,64,128]{3,2,1,0:T(8,128)} %get-tuple-element.34), calls=%async_computation.1 | async-start | bytes 23068672 | tf_op jit(solution)/shard_map/all_to_all | solution.py:282
  140.7 7.6 %collective-permute-start.7 = (f32[64,128,128]{2,1,0:T(8,128)}, f32[64,128,128]{2,1,0:T(8,128)}, u32[]{:S(2)}, u32[]{:S(2)}) collective-permute-start(f32[64,128,128]{2,1,0:T(8,128)} %get-tuple-element.25), channel_id=1, source_target_pairs={{0,1},{1,0},{2,3},{3,2},{4,5},{5,4},{6,7},{7,6},{8,9},{9,8},{10,11... | collective-permute-start | bytes 12582920 | tf_op jit(solution)/shard_map/ppermute | solution.py:279
  140.7 93.8 %collective-permute-start.8 = (f32[64,128,128]{2,1,0:T(8,128)}, f32[64,128,128]{2,1,0:T(8,128)}, u32[]{:S(2)}, u32[]{:S(2)}) collective-permute-start(f32[64,128,128]{2,1,0:T(8,128)} %get-tuple-element.26), channel_id=1, source_target_pairs={{0,2},{1,3},{2,0},{3,1},{4,6},{5,7},{6,4},{7,5},{8,10},{9,11},{10,... | collective-permute-start | bytes 12582920 | tf_op jit(solution)/shard_map/ppermute | solution.py:279
  142.3 181.1 %collective-permute-start.9 = (f32[64,128,128]{2,1,0:T(8,128)}, f32[64,128,128]{2,1,0:T(8,128)}, u32[]{:S(2)}, u32[]{:S(2)}) collective-permute-start(f32[64,128,128]{2,1,0:T(8,128)} %get-tuple-element.27), channel_id=1, source_target_pairs={{0,3},{1,2},{2,1},{3,0},{4,7},{5,6},{6,5},{7,4},{8,11},{9,10},{10,... | collective-permute-start | bytes 12582920 | tf_op jit(solution)/shard_map/ppermute | solution.py:279
  323.5 2.2 copy-start
  389.8 30.0 %all-to-all-start.2 = ((f32[8,4,64,128]{3,2,1,0:T(8,128)}), f32[8,4,64,128]{3,2,1,0:T(8,128)S(1)}, u32[]{:S(2)}, u32[]{:S(2)}) async-start(f32[8,4,64,128]{3,2,1,0:T(8,128)} %get-tuple-element.36), calls=%async_computation.2 | async-start | bytes 2097152 | tf_op jit(solution)/shard_map/all_to_all | solution.py:282
  393.9 1.2 copy-start.1
  419.8 1.2 copy-start.2
  426.6 2.0 collective-permute-start.10
  429.7 8.4 %collective-permute-start.11 = (f32[1,512,128]{2,1,0:T(8,128)S(1)}, f32[1,512,128]{2,1,0:T(8,128)S(1)}, u32[]{:S(2)}, u32[]{:S(2)}) collective-permute-start(f32[1,512,128]{2,1,0:T(8,128)S(1)} %constant_dynamic-slice_fusion), channel_id=1, source_target_pairs={{0,2},{1,3},{2,0},{3,1},{4,6},{5,7},{6,4},{7,5},{8,10},{9,11},{10,... | collective-permute-start | bytes 786440 | tf_op jit(solution)/shard_map/ppermute | solution.py:279

commit v3 on v2

--- a/solution.py
+++ b/solution.py
@@ -47,10 +47,9 @@
     )
 
 
-def second_kernel(peers, tile, per_dot, k_ref, *refs):
-    count = (len(refs) - 2) // 2
-    d_refs, out_refs = refs[:count], refs[count : 2 * count]
-    rows, both = refs[2 * count :]
+def second_kernel(peers, count, tile, per_dot, k_ref, *refs):
+    d_refs, out_refs = refs[:count], refs[-2 - count : -2]
+    rows, both = refs[-2:]
     nc = k_ref.shape[2]
     depth = k_ref.shape[3]
     width = both.shape[0] // 2
@@ -77,22 +76,27 @@
                 out_ref[peer, b, :, :] = rows[pl.ds(from_row, tile, stride=width), :]
 
 
-def second(integrals, d_rows, peers):
+def second(integrals, d_rows, peers, a0, count_a, into=()):
     heights = tuple(d.shape[0] for d in d_rows)
     width = sum(heights)
     na, nc, depth = integrals.shape[1:]
     tile = 8
     per_dot = max(1, WIDE // nc)
-    flops = 6 * width * na * nc * depth
-    size = 4 * (na * nc * depth + width * na * nc)
+    flops = 6 * width * count_a * nc * depth
+    size = 4 * (count_a * nc * depth + width * count_a * nc)
+    at = a0 // tile
+    count = len(d_rows)
     return pl.pallas_call(
-        functools.partial(second_kernel, peers, tile, per_dot),
-        grid=(na // tile,),
-        in_specs=[pl.BlockSpec((1, tile, nc, depth), lambda s: (0, s, 0, 0))]
-        + [pl.BlockSpec((h, depth), lambda s: (0, 0)) for h in heights],
+        functools.partial(second_kernel, peers, count, tile, per_dot),
+        grid=(count_a // tile,),
+        in_specs=[pl.BlockSpec((1, tile, nc, depth), lambda s: (0, s + at, 0, 0))]
+        + [pl.BlockSpec((h, depth), lambda s: (0, 0)) for h in heights]
+        + [pl.BlockSpec(memory_space=pl.ANY) for _ in into],
         out_specs=[
-            pl.BlockSpec((peers, h // peers, tile, nc), lambda s: (0, 0, s, 0)) for h in heights
+            pl.BlockSpec((peers, h // peers, tile, nc), lambda s: (0, 0, s + at, 0))
+            for h in heights
         ],
+        input_output_aliases={1 + count + q: q for q in range(len(into))},
         out_shape=[pltpu.HBM((peers, h // peers, na, nc), F32) for h in heights],
         scratch_shapes=[
             pltpu.VMEM((tile * width, nc), F32),
@@ -100,7 +104,7 @@
         ],
         name="second",
         **params(flops, size),
-    )(integrals, *d_rows)
+    )(integrals, *d_rows, *into)
 
 
 def third_kernel(i_ref, d_ref, *refs):
@@ -246,7 +250,7 @@
             pltpu.HBM((base.shape[0], nc, total), F32),
             pltpu.HBM((depth // nc, total, nc), F32),
         ],
-        input_output_aliases={6: 0} if given else {},
+        input_output_aliases={6: 0, 7: 1} if given else {},
         name="finish",
         **params(flops, size),
     )(eb, ec, ea, integrals, base, blocks, *given)
@@ -294,20 +298,21 @@
 
     share = depth // m
     own = doubles[1][: lots[0]]
-    own = jnp.concatenate([own[:, q * share : (q + 1) * share] for q in range(m)])
     part = lax.dynamic_slice_in_dim(doubles, j * share, share, axis=2)
-    head = jnp.concatenate([own, part.reshape(3 * nb, share)])
-    head = jnp.stack([over_b(head, k) for k in range(0, n, 2)])
+    far_rows = jnp.stack([over_b(own, k) for k in range(0, n, 2)])
+    far_part = jnp.stack([over_b(part, k) for k in range(0, n, 2)])
 
     def from_last_bit(x):
         x = jnp.stack([x, over_b(x, 1)], axis=1)
         x = x.reshape((n,) + x.shape[2:])
         return jnp.stack([lax.dynamic_index_in_dim(x, i ^ p, 0, False) for p in range(n)])
 
-    rows = from_last_bit(head[:, : m * lots[0]]).reshape(n, m, lots[0], share)
-    rows = jnp.concatenate([rows[:, q] for q in range(m)], axis=2).reshape(n * lots[0], depth)
-    part = from_last_bit(tie(head[:, m * lots[0] :], rows))
-    (lot,) = second(integrals, (rows,), n)
+    rows = from_last_bit(far_rows).reshape(n * lots[0], depth)
+    half = nb // 2
+    begun = second(integrals, (rows,), n, 0, half)
+    far_part, begun = lax.optimization_barrier((far_part, tuple(begun)))
+    part = from_last_bit(far_part)
+    (lot,) = second(integrals, (rows,), n, half, nb - half, begun)
     part, lot = lax.optimization_barrier((part, lot))
     arrived = [all_over_b(lot)]
 
@@ -327,7 +332,7 @@
         by_peer[:, at : at + lot].reshape(n * lot, depth)
         for at, lot in zip(starts[1:], lots[1:])
     ]
-    made = second(integrals, tie(tuple(rows), *thirds), n)
+    made = second(integrals, tie(tuple(rows), *thirds), n, 0, nb)
     thirds = [over_c(x, q) for q, x in enumerate(thirds)]
     made = tie(tuple(made), arrived[0])
     arrived.append(all_over_b(made[0]))

time: 453 us -> 451 us (level)
  waiting for transfers between devices: 271 us -> 265 us
    ppermute x5 -> x8, waiting for transfers between devices: 13.8 us -> 5.73 us  [over_b(): return lax.ppermute(x, 'vb', [(p, p ^ k) for p in range(n)]) if k else x]
    ppermute x5 -> x8, starting transfers between devices: 8.87 us -> 13.3 us  [over_b(): return lax.ppermute(x, 'vb', [(p, p ^ k) for p in range(n)]) if k else x]
    pallas_call x2 -> x3, Pallas kernels: 34.9 us -> 36.5 us  [second(): pl.pallas_call(functools.partial(second_kernel, peers, count, tile, per_d...]
  transfers between devices with their start and end apart: 15 -> 18, of which waited for: 13 -> 13; matrix products, arithmetic and copies ran while one was open for 2% -> 2% of each run, Pallas kernels for 26% -> 25%
where the time goes in v3:
time: 451 us; the launch traced here: 449 us
  waiting for transfers between devices  265 us (59%)
  Pallas kernels  124 us (27%)
  starting transfers between devices  32.5 us (7%)
  blocking collectives  12 us (3%)
  local copies, waits for them, and re-layouts  9.39 us (2%)
  other arithmetic  5.76 us (1%)
    ppermute x7, waiting for transfers between devices, over_c(): return lax.ppermute(x, 'vc', [(p, p ^ k) for p in range(m)]) if k else x  208 us
    all_to_all x3, waiting for transfers between devices, all_over_b(): return lax.all_to_all(x, 'vb', split_axis=0, concat_axis=0, tiled=True)  51.2 us
    pallas_call x3, Pallas kernels, finish(): pl.pallas_call(functools.partial(finish_kernel, b0), grid_spec=pltpu.Pref...  37.6 us
    pallas_call x3, Pallas kernels, second(): pl.pallas_call(functools.partial(second_kernel, peers, count, tile, per_d...  36.5 us
    pallas_call x1, Pallas kernels, first(): pl.pallas_call(functools.partial(first_kernel, per_dot), grid_spec=pltpu....  26.7 us
    pallas_call x1, Pallas kernels, third(): pl.pallas_call(third_kernel, grid=(nb // tile,), in_specs=[pl.BlockSpec((...  23.2 us
    all_to_all x3, starting transfers between devices, all_over_b(): return lax.all_to_all(x, 'vb', split_axis=0, concat_axis=0, tiled=True)  14 us
    ppermute x8, starting transfers between devices, over_b(): return lax.ppermute(x, 'vb', [(p, p ^ k) for p in range(n)]) if k else x  13.3 us
  transfers between devices with their start and end apart: 18, of which 13 were waited for; matrix products, arithmetic and copies ran while one was open for 2% of the time, Pallas kernels for 25%

profile of v3, /device:TPU:0, one launch (start us, length us, event | category | flops | bytes accessed | tf_op | source)
XLA Modules:
  0.0 449.3 jit_solution(14018737779519774176)
XLA Ops:
  0.6 0.8 fusion.3
  1.4 5.0 %collective-permute-start.5 = (f32[16,512]{1,0:T(8,128)S(1)}, f32[16,512]{1,0:T(8,128)S(1)}, u32[]{:S(2)}, u32[]{:S(2)}) collective-permute-start(f32[16,512]{1,0:T(8,128)S(1)} %get-tuple-element.58), channel_id=1, source_target_pairs={{0,24},{4,28},{8,16},{12,20},{16,8},{20,12},{24,0},{28,4},{1,25},{... | collective-permute-start | bytes 98312 | tf_op jit(solution)/shard_map/ppermute | solution.py:280
  6.4 0.6 collective-permute-start.3
  7.0 0.9 constant_dynamic-slice_fusion.1
  7.9 3.8 collective-permute-start.2
  11.7 0.6 collective-permute-start
  12.4 1.7 collective-permute-start.6
  14.1 0.9 fusion.4
  15.2 4.3 collective-permute-done.1
  19.7 7.7 %second.3.refs_1_ = f32[8,16,64,128]{3,2,1,0:T(8,128)} custom-call(f32[2,64,128,512]{3,2,1,0:T(8,128)} %k_ref.13, f32[128,512]{1,0:T(8,128)S(1)} %bitcast.61), custom_call_target="tpu_custom_call" | custom-call | flops 1610612 | bytes 10485 | tf_op jit(solution)/shard_map/second/pallas_call | solution.py:89
  27.4 1.5 collective-permute-start.7
  28.9 7.7 %second.4 = f32[8,16,64,128]{3,2,1,0:T(8,128)} custom-call(f32[2,64,128,512]{3,2,1,0:T(8,128)} %k_ref.13, f32[128,512]{1,0:T(8,128)S(1)} %bitcast.62, f32[8,16,64,128]{3,2,1,0:T(8,128)} %second.3.refs_1_), custom_call_target="tpu_custom_call", output_to_operand_aliasing={{}: (2, {})} | custom-call | flops 1610612 | bytes 10485 | tf_op jit(solution)/shard_map/second/pallas_call | solution.py:89
  36.5 1.3 collective-permute-done.7
  38.1 4.6 %all-to-all-start = ((f32[8,16,64,128]{3,2,1,0:T(8,128)}), f32[8,16,64,128]{3,2,1,0:T(8,128)}, u32[]{:S(2)}, u32[]{:S(2)}) async-start(f32[8,16,64,128]{3,2,1,0:T(8,128)} %second.4), calls=%async_computation | async-start | bytes 8388608 | tf_op jit(solution)/shard_map/all_to_all | solution.py:286
  42.7 1.6 collective-permute-start.8
  44.3 16.4 %collective-permute-done.8 = f32[3,512,128]{2,1,0:T(8,128)S(1)} collective-permute-done((f32[3,512,128]{2,1,0:T(8,128)S(1)}, f32[3,512,128]{2,1,0:T(8,128)S(1)}, u32[]{:S(2)}, u32[]{:S(2)}) %collective-permute-start.8) | collective-permute-done | bytes 786464 | tf_op jit(solution)/shard_map/ppermute | solution.py:283
  60.7 0.3 fusion.1
  61.1 3.5 collective-permute-done.9
  64.6 1.6 pad_maximum_fusion
  66.9 0.3 fusion.2
  67.2 0.9 slice.41
  68.1 1.2 reshape.49.refs_0_
  69.6 23.2 %third.1 = (f32[64,128,128]{2,1,0:T(8,128)}, f32[64,128,128]{2,1,0:T(8,128)}, f32[64,128,128]{2,1,0:T(8,128)}, f32[64,128,128]{2,1,0:T(8,128)}) custom-call(f32[2,64,128,512]{3,2,1,0:T(8,128)} %k_ref.13, f32[512,512]{1,0:T(8,128)S(1)} %pad_maximum_fusion.3.d_ref), custom_call_target="tpu_custom_call" | custom-call | flops 12884901 | bytes 33554 | tf_op jit(solution)/shard_map/third/pallas_call | solution.py:133
  92.8 21.1 %second.5 = (f32[8,44,64,128]{3,2,1,0:T(8,128)}, f32[8,4,64,128]{3,2,1,0:T(8,128)}) custom-call(f32[2,64,128,512]{3,2,1,0:T(8,128)} %k_ref.13, f32[352,512]{1,0:T(8,128)S(1)} %reshape.49.refs_0_, f32[32,512]{1,0:T(8,128)S(1)} %reshape.50.refs_1_), custom_call_target="tpu_custom_call" | custom-call | flops 9663676 | bytes 29360 | tf_op jit(solution)/shard_map/second/pallas_call | solution.py:89
  113.9 20.8 %all-to-all-done.t_ref = f32[8,16,64,128]{3,2,1,0:T(8,128)} async-done(((f32[8,16,64,128]{3,2,1,0:T(8,128)}), f32[8,16,64,128]{3,2,1,0:T(8,128)}, u32[]{:S(2)}, u32[]{:S(2)}) %all-to-all-start) | async-done | bytes 4194336 | tf_op jit(solution)/shard_map/all_to_all | solution.py:286
  134.8 5.4 %all-to-all-start.1 = ((f32[8,44,64,128]{3,2,1,0:T(8,128)}), f32[8,44,64,128]{3,2,1,0:T(8,128)}, u32[]{:S(2)}, u32[]{:S(2)}) async-start(f32[8,44,64,128]{3,2,1,0:T(8,128)} %get-tuple-element.36), calls=%async_computation.1 | async-start | bytes 23068672 | tf_op jit(solution)/shard_map/all_to_all | solution.py:286
  140.2 1.6 collective-permute-start.11
  141.8 0.3 collective-permute-start.12
  142.4 0.7 select_reduce_fusion.1
  143.1 0.7 dynamic-slice_subtract_fusion.eb_ref
  143.9 3.8 collective-permute-done.10.refs_1_
  147.7 86.3 %collective-permute-done.11.refs_2_ = f32[64,128,128]{2,1,0:T(8,128)} collective-permute-done((f32[64,128,128]{2,1,0:T(8,128)}, f32[64,128,128]{2,1,0:T(8,128)}, u32[]{:S(2)}, u32[]{:S(2)}) %collective-permute-start.11) | collective-permute-done | bytes 4194336 | tf_op jit(solution)/shard_map/ppermute | solution.py:283
  234.0 89.0 %collective-permute-done.12.refs_3_ = f32[64,128,128]{2,1,0:T(8,128)} collective-permute-done((f32[64,128,128]{2,1,0:T(8,128)}, f32[64,128,128]{2,1,0:T(8,128)}, u32[]{:S(2)}, u32[]{:S(2)}) %collective-permute-start.12) | collective-permute-done | bytes 4194336 | tf_op jit(solution)/shard_map/ppermute | solution.py:283
  323.0 2.2 copy-done
  325.2 26.7 %first.1.q_ref = f32[64,512,128]{2,1,0:T(8,128)} custom-call(s32[4]{0:T(128)S(1)} %pad_add_fusion.off_ref, f32[2,64,128,512]{3,2,1,0:T(8,128)} %k_ref.13, f32[512,512]{1,0:T(8,128)S(1)} %get-tuple-element.46.d_ref, f32[64,128,128]{2,1,0:T(8,128)S(1)} %copy-done, f32[64,128,128]{2,1,0:T(8,128)} %collective-permute-done.10.refs_1_, ...), custom_call_target="tpu_custom_call" | custom-call | flops 12884901 | bytes 50331 | tf_op jit(solution)/shard_map/first/pallas_call | solution.py:178
  352.0 9.5 %finish.3 = (f32[64,128,512]{2,1,0:T(8,128)}, f32[4,512,128]{2,1,0:T(8,128)}) custom-call(f32[64]{0:T(128)S(1)} %dynamic-slice_subtract_fusion.eb_ref, f32[1,128]{1,0:T(1,128)S(1)} %dynamic-slice_bitcast_fusion.9.ec_ref, f32[512,128]{1,0:T(8,128)S(1)} %broadcast_in_dim.44.ea_ref, f32[2,64,128,512]{3,2,1,0:T(8,128)} %k_ref.13, f32[64,512,128]{2,1,0:T(8,128)} %first.1.q_ref, ...), custom_call_target="tpu_custom_call" | custom-call | flops 3221225 | bytes 16777 | tf_op jit(solution)/shard_map/finish/pallas_call | solution.py:228
  361.6 27.7 %all-to-all-done.1.t_ref = f32[8,44,64,128]{3,2,1,0:T(8,128)} async-done(((f32[8,44,64,128]{3,2,1,0:T(8,128)}), f32[8,44,64,128]{3,2,1,0:T(8,128)}, u32[]{:S(2)}, u32[]{:S(2)}) %all-to-all-start.1) | async-done | bytes 11534368 | tf_op jit(solution)/shard_map/all_to_all | solution.py:286
  389.3 4.1 all-to-all-start.2
  393.3 23.3 %finish.4 = (f32[64,128,512]{2,1,0:T(8,128)}, f32[4,512,128]{2,1,0:T(8,128)}) custom-call(f32[64]{0:T(128)S(1)} %dynamic-slice_subtract_fusion.eb_ref, f32[1,128]{1,0:T(1,128)S(1)} %dynamic-slice_bitcast_fusion.9.ec_ref, f32[512,128]{1,0:T(8,128)S(1)} %broadcast_in_dim.44.ea_ref, ...), custom_call_target="tpu_custom_call", output_to_operand_aliasing={{0}: (6, {}), {1}: (7, {})} | custom-call | flops 8858370 | bytes 46137 | tf_op jit(solution)/shard_map/finish/pallas_call | solution.py:228
  416.7 2.6 all-to-all-done.2.t_ref
  419.3 4.7 %finish.5 = (f32[64,128,512]{2,1,0:T(8,128)}, f32[4,512,128]{2,1,0:T(8,128)}) custom-call(f32[64]{0:T(128)S(1)} %dynamic-slice_subtract_fusion.eb_ref, f32[1,128]{1,0:T(1,128)S(1)} %dynamic-slice_bitcast_fusion.9.ec_ref, f32[512,128]{1,0:T(8,128)S(1)} %broadcast_in_dim.44.ea_ref, ...), custom_call_target="tpu_custom_call", output_to_operand_aliasing={{0}: (6, {}), {1}: (7, {})} | custom-call | flops 805306 | bytes 4194 | tf_op jit(solution)/shard_map/finish/pallas_call | solution.py:228
  424.0 1.1 dynamic-slice_bitcast_fusion.4
  425.2 1.9 collective-permute-done.13
  427.1 1.1 bitcast_add_fusion
  428.2 1.6 collective-permute-start.14
  429.8 6.8 %collective-permute-done.14 = f32[1,512,128]{2,1,0:T(8,128)S(1)} collective-permute-done((f32[1,512,128]{2,1,0:T(8,128)S(1)}, f32[1,512,128]{2,1,0:T(8,128)S(1)}, u32[]{:S(2)}, u32[]{:S(2)}) %collective-permute-start.14) | collective-permute-done | bytes 262176 | tf_op jit(solution)/shard_map/ppermute | solution.py:283
  436.7 12.0 %all_to_all.20 = f32[8,64,128]{2,1,0:T(8,128)S(1)} all-to-all(f32[8,64,128]{2,1,0:T(8,128)S(1)} %bitcast.87), channel_id=1, replica_groups=mesh['vb'=8,'vc'=4] {'vb'}, dimensions={0} | all-to-all | bytes 524288 | tf_op jit(solution)/shard_map/all_to_all | solution.py:286
  448.6 0.6 reduce_sum.29
  (54 shorter events, 2.3 us)
Async XLA Ops:
  1.4 10.3 %collective-permute-start.5 = (f32[16,512]{1,0:T(8,128)S(1)}, f32[16,512]{1,0:T(8,128)S(1)}, u32[]{:S(2)}, u32[]{:S(2)}) collective-permute-start(f32[16,512]{1,0:T(8,128)S(1)} %get-tuple-element.58), channel_id=1, source_target_pairs={{0,24},{4,28},{8,16},{12,20},{16,8},{20,12},{24,0},{28,4},{1,25},{... | collective-permute-start | bytes 98312 | tf_op jit(solution)/shard_map/ppermute | solution.py:280
  6.4 5.9 %collective-permute-start.4 = (f32[16,512]{1,0:T(8,128)S(1)}, f32[16,512]{1,0:T(8,128)S(1)}, u32[]{:S(2)}, u32[]{:S(2)}) collective-permute-start(f32[16,512]{1,0:T(8,128)S(1)} %get-tuple-element.58), channel_id=1, source_target_pairs={{0,16},{4,20},{8,24},{12,28},{16,0},{20,4},{24,8},{28,12},{1,17},{... | collective-permute-start | bytes 98312 | tf_op jit(solution)/shard_map/ppermute | solution.py:280
  6.4 5.9 %collective-permute-start.3 = (f32[16,512]{1,0:T(8,128)S(1)}, f32[16,512]{1,0:T(8,128)S(1)}, u32[]{:S(2)}, u32[]{:S(2)}) collective-permute-start(f32[16,512]{1,0:T(8,128)S(1)} %get-tuple-element.58), channel_id=1, source_target_pairs={{0,8},{4,12},{8,0},{12,4},{16,24},{20,28},{24,16},{28,20},{1,9},{5... | collective-permute-start | bytes 98312 | tf_op jit(solution)/shard_map/ppermute | solution.py:280
  7.9 7.2 %collective-permute-start.2 = (f32[3,64,128]{2,1,0:T(8,128)S(1)}, f32[3,64,128]{2,1,0:T(8,128)S(1)}, u32[]{:S(2)}, u32[]{:S(2)}) collective-permute-start(f32[3,64,128]{2,1,0:T(8,128)S(1)} %constant_dynamic-slice_fusion.1), channel_id=1, source_target_pairs={{0,24},{4,28},{8,16},{12,20},{16,8},{20,12},{24,0},{28,4},{1,25},{... | collective-permute-start | bytes 294920 | tf_op jit(solution)/shard_map/ppermute | solution.py:280
  11.7 7.7 %collective-permute-start.1 = (f32[3,64,128]{2,1,0:T(8,128)S(1)}, f32[3,64,128]{2,1,0:T(8,128)S(1)}, u32[]{:S(2)}, u32[]{:S(2)}) collective-permute-start(f32[3,64,128]{2,1,0:T(8,128)S(1)} %constant_dynamic-slice_fusion.1), channel_id=1, source_target_pairs={{0,16},{4,20},{8,24},{12,28},{16,0},{20,4},{24,8},{28,12},{1,17},{... | collective-permute-start | bytes 294920 | tf_op jit(solution)/shard_map/ppermute | solution.py:280
  11.7 7.7 %collective-permute-start = (f32[3,64,128]{2,1,0:T(8,128)S(1)}, f32[3,64,128]{2,1,0:T(8,128)S(1)}, u32[]{:S(2)}, u32[]{:S(2)}) collective-permute-start(f32[3,64,128]{2,1,0:T(8,128)S(1)} %constant_dynamic-slice_fusion.1), channel_id=1, source_target_pairs={{0,8},{4,12},{8,0},{12,4},{16,24},{20,28},{24,16},{28,20},{1,9},{5... | collective-permute-start | bytes 294920 | tf_op jit(solution)/shard_map/ppermute | solution.py:280
  12.4 7.1 %collective-permute-start.6 = (f32[4,16,512]{2,1,0:T(8,128)S(1)}, f32[4,16,512]{2,1,0:T(8,128)S(1)}, u32[]{:S(2)}, u32[]{:S(2)}) collective-permute-start(f32[4,16,512]{2,1,0:T(8,128)S(1)} %get-tuple-element.60), channel_id=1, source_target_pairs={{0,4},{4,0},{8,12},{12,8},{16,20},{20,16},{24,28},{28,24},{1,5},{5... | collective-permute-start | bytes 393224 | tf_op jit(solution)/shard_map/ppermute | solution.py:280
  27.4 10.4 %collective-permute-start.7 = (f32[4,3,64,128]{3,2,1,0:T(8,128)S(1)}, f32[4,3,64,128]{3,2,1,0:T(8,128)S(1)}, u32[]{:S(2)}, u32[]{:S(2)}) collective-permute-start(f32[4,3,64,128]{3,2,1,0:T(8,128)S(1)} %pad_maximum_fusion.5), channel_id=1, source_target_pairs={{0,4},{4,0},{8,12},{12,8},{16,20},{20,16},{24,28},{28,24},{1,5},{5... | collective-permute-start | bytes 1179656 | tf_op jit(solution)/shard_map/ppermute | solution.py:280
  38.1 96.7 %all-to-all-start = ((f32[8,16,64,128]{3,2,1,0:T(8,128)}), f32[8,16,64,128]{3,2,1,0:T(8,128)}, u32[]{:S(2)}, u32[]{:S(2)}) async-start(f32[8,16,64,128]{3,2,1,0:T(8,128)} %second.4), calls=%async_computation | async-start | bytes 8388608 | tf_op jit(solution)/shard_map/all_to_all | solution.py:286
  42.7 18.0 %collective-permute-start.8 = (f32[3,512,128]{2,1,0:T(8,128)S(1)}, f32[3,512,128]{2,1,0:T(8,128)S(1)}, u32[]{:S(2)}, u32[]{:S(2)}) collective-permute-start(f32[3,512,128]{2,1,0:T(8,128)S(1)} %bitcast.76), channel_id=1, source_target_pairs={{0,2},{1,3},{2,0},{3,1},{4,6},{5,7},{6,4},{7,5},{8,10},{9,11},{10,... | collective-permute-start | bytes 2359304 | tf_op jit(solution)/shard_map/ppermute | solution.py:283
  61.0 3.6 collective-permute-start.9
  134.7 7.4 %copy-start.1 = (f32[512]{0:T(512)S(1)}, f32[512]{0:T(512)}, u32[]{:S(2)}) copy-start(f32[512]{0:T(512)} %param.9) | copy-start | bytes 6148
  134.7 7.4 %copy-start.2 = (s32[512]{0:T(512)S(1)}, s32[512]{0:T(512)}, u32[]{:S(2)}) copy-start(s32[512]{0:T(512)} %param.11) | copy-start | bytes 6148
  134.7 7.7 %copy-start.3 = (f32[100]{0:T(128)S(1)}, f32[100]{0:T(128)}, u32[]{:S(2)}) copy-start(f32[100]{0:T(128)} %param.8) | copy-start | bytes 1204
  134.7 7.7 %copy-start.4 = (s32[3]{0:T(128)S(1)}, s32[3]{0:T(128)}, u32[]{:S(2)}) copy-start(s32[3]{0:T(128)} %param.10) | copy-start | bytes 40
  134.8 254.5 %all-to-all-start.1 = ((f32[8,44,64,128]{3,2,1,0:T(8,128)}), f32[8,44,64,128]{3,2,1,0:T(8,128)}, u32[]{:S(2)}, u32[]{:S(2)}) async-start(f32[8,44,64,128]{3,2,1,0:T(8,128)} %get-tuple-element.36), calls=%async_computation.1 | async-start | bytes 23068672 | tf_op jit(solution)/shard_map/all_to_all | solution.py:286
  140.2 7.6 %collective-permute-start.10 = (f32[64,128,128]{2,1,0:T(8,128)}, f32[64,128,128]{2,1,0:T(8,128)}, u32[]{:S(2)}, u32[]{:S(2)}) collective-permute-start(f32[64,128,128]{2,1,0:T(8,128)} %get-tuple-element.27), channel_id=1, source_target_pairs={{0,1},{1,0},{2,3},{3,2},{4,5},{5,4},{6,7},{7,6},{8,9},{9,8},{10,11... | collective-permute-start | bytes 12582920 | tf_op jit(solution)/shard_map/ppermute | solution.py:283
  140.2 93.8 %collective-permute-start.11 = (f32[64,128,128]{2,1,0:T(8,128)}, f32[64,128,128]{2,1,0:T(8,128)}, u32[]{:S(2)}, u32[]{:S(2)}) collective-permute-start(f32[64,128,128]{2,1,0:T(8,128)} %get-tuple-element.28), channel_id=1, source_target_pairs={{0,2},{1,3},{2,0},{3,1},{4,6},{5,7},{6,4},{7,5},{8,10},{9,11},{10,... | collective-permute-start | bytes 12582920 | tf_op jit(solution)/shard_map/ppermute | solution.py:283
  141.8 181.1 %collective-permute-start.12 = (f32[64,128,128]{2,1,0:T(8,128)}, f32[64,128,128]{2,1,0:T(8,128)}, u32[]{:S(2)}, u32[]{:S(2)}) collective-permute-start(f32[64,128,128]{2,1,0:T(8,128)} %get-tuple-element.29), channel_id=1, source_target_pairs={{0,3},{1,2},{2,1},{3,0},{4,7},{5,6},{6,5},{7,4},{8,11},{9,10},{10,... | collective-permute-start | bytes 12582920 | tf_op jit(solution)/shard_map/ppermute | solution.py:283
  323.0 2.2 copy-start
  389.3 30.0 %all-to-all-start.2 = ((f32[8,4,64,128]{3,2,1,0:T(8,128)}), f32[8,4,64,128]{3,2,1,0:T(8,128)S(1)}, u32[]{:S(2)}, u32[]{:S(2)}) async-start(f32[8,4,64,128]{3,2,1,0:T(8,128)} %get-tuple-element.38), calls=%async_computation.2 | async-start | bytes 2097152 | tf_op jit(solution)/shard_map/all_to_all | solution.py:286
  425.1 2.0 collective-permute-start.13
  428.2 8.4 %collective-permute-start.14 = (f32[1,512,128]{2,1,0:T(8,128)S(1)}, f32[1,512,128]{2,1,0:T(8,128)S(1)}, u32[]{:S(2)}, u32[]{:S(2)}) collective-permute-start(f32[1,512,128]{2,1,0:T(8,128)S(1)} %constant_dynamic-slice_fusion), channel_id=1, source_target_pairs={{0,2},{1,3},{2,0},{3,1},{4,6},{5,7},{6,4},{7,5},{8,10},{9,11},{10,... | collective-permute-start | bytes 786440 | tf_op jit(solution)/shard_map/ppermute | solution.py:283

commit v4 on v3

--- a/solution.py
+++ b/solution.py
@@ -350,18 +350,17 @@
         given = finish(integrals, base, blocks, eb, ec, ea, at, given)
     amplitudes, grad = given
 
-    step = 1
-    while step < m:
-        bit = (j // step) % 2
-        pairs = grad.reshape(-1, 2, total, nc)
-        keep = lax.dynamic_index_in_dim(pairs, bit, 1, False)
-        give = lax.dynamic_index_in_dim(pairs, 1 - bit, 1, False)
-        grad = keep + over_c(give, step)
-        step *= 2
-    grad = grad.reshape(total, nc)
-
-    grad = jnp.sum(all_over_b(grad.reshape(n, nb, nc)), axis=0)
-    return amplitudes, grad
+    bit = j % 2
+    pairs = grad.reshape(-1, 2, total, nc)
+    keep = lax.dynamic_index_in_dim(pairs, bit, 1, False)
+    give = lax.dynamic_index_in_dim(pairs, 1 - bit, 1, False)
+    grad = keep + over_c(give, 1)
+    grad = grad.reshape(m // 2, n, nb, nc).transpose(1, 0, 2, 3).reshape(n * m // 2, nb, nc)
+    alike = [[p * m + q for p in range(n) for q in range(c, m, 2)] for c in range(2)]
+    grad = lax.all_to_all(
+        grad, ("vb", "vc"), split_axis=0, concat_axis=0, axis_index_groups=alike, tiled=True
+    )
+    return amplitudes, jnp.sum(grad, axis=0)
 
 
 def plain(integrals, doubles, eps_occ, eps_virt, triple, energy_order):

time: 451 us -> 449 us (level)
  waiting for transfers between devices: 265 us -> 255 us
  blocking collectives: 12 us -> 19.9 us
    all_to_all x1, blocking collectives: 12 us -> 19.9 us  [in_blocks(): lax.all_to_all(grad, ('vb', 'vc'), split_axis=0, concat_axis=0, axis_inde...]
    ppermute x7 -> x6, waiting for transfers between devices: 208 us -> 200 us  [over_c(): return lax.ppermute(x, 'vc', [(p, p ^ k) for p in range(m)]) if k else x]
  transfers between devices with their start and end apart: 18 -> 17, of which waited for: 13 -> 12; matrix products, arithmetic and copies ran while one was open for 2% -> 2% of each run, Pallas kernels for 25% -> 25%
where the time goes in v4:
time: 449 us; the launch traced here: 448 us
  waiting for transfers between devices  255 us (57%)
  Pallas kernels  124 us (28%)
  starting transfers between devices  32.1 us (7%)
  blocking collectives  19.9 us (4%)
  local copies, waits for them, and re-layouts  9.4 us (2%)
  other arithmetic  5.75 us (1%)
    ppermute x6, waiting for transfers between devices, over_c(): return lax.ppermute(x, 'vc', [(p, p ^ k) for p in range(m)]) if k else x  200 us
    all_to_all x3, waiting for transfers between devices, all_over_b(): return lax.all_to_all(x, 'vb', split_axis=0, concat_axis=0, tiled=True)  51.3 us
    pallas_call x3, Pallas kernels, finish(): pl.pallas_call(functools.partial(finish_kernel, b0), grid_spec=pltpu.Pref...  37.6 us
    pallas_call x3, Pallas kernels, second(): pl.pallas_call(functools.partial(second_kernel, peers, count, tile, per_d...  36.5 us
    pallas_call x1, Pallas kernels, first(): pl.pallas_call(functools.partial(first_kernel, per_dot), grid_spec=pltpu....  26.7 us
    pallas_call x1, Pallas kernels, third(): pl.pallas_call(third_kernel, grid=(nb // tile,), in_specs=[pl.BlockSpec((...  23.2 us
    all_to_all x1, blocking collectives, in_blocks(): lax.all_to_all(grad, ('vb', 'vc'), split_axis=0, concat_axis=0, axis_inde...  19.9 us
    all_to_all x3, starting transfers between devices, all_over_b(): return lax.all_to_all(x, 'vb', split_axis=0, concat_axis=0, tiled=True)  15.2 us
  transfers between devices with their start and end apart: 17, of which 12 were waited for; matrix products, arithmetic and copies ran while one was open for 2% of the time, Pallas kernels for 25%

profile of v4, /device:TPU:0, one launch (start us, length us, event | category | flops | bytes accessed | tf_op | source)
XLA Modules:
  0.0 447.6 jit_solution(18309669616541564668)
XLA Ops:
  0.6 0.8 fusion.3
  1.4 5.0 %collective-permute-start.5 = (f32[16,512]{1,0:T(8,128)S(1)}, f32[16,512]{1,0:T(8,128)S(1)}, u32[]{:S(2)}, u32[]{:S(2)}) collective-permute-start(f32[16,512]{1,0:T(8,128)S(1)} %get-tuple-element.58), channel_id=1, source_target_pairs={{0,24},{4,28},{8,16},{12,20},{16,8},{20,12},{24,0},{28,4},{1,25},{... | collective-permute-start | bytes 98312 | tf_op jit(solution)/shard_map/ppermute | solution.py:280
  6.4 0.6 collective-permute-start.3
  7.0 0.9 constant_dynamic-slice_fusion
  7.9 2.4 collective-permute-start.1
  10.3 2.0 collective-permute-start
  12.3 1.8 collective-permute-start.6
  14.1 0.9 fusion.4
  15.0 1.7 collective-permute-done.1
  16.7 2.1 collective-permute-done.2
  19.0 7.7 %second.3.refs_1_ = f32[8,16,64,128]{3,2,1,0:T(8,128)} custom-call(f32[2,64,128,512]{3,2,1,0:T(8,128)} %k_ref.13, f32[128,512]{1,0:T(8,128)S(1)} %bitcast.64), custom_call_target="tpu_custom_call" | custom-call | flops 1610612 | bytes 10485 | tf_op jit(solution)/shard_map/second/pallas_call | solution.py:89
  26.7 1.5 collective-permute-start.7
  28.2 7.7 %second.4 = f32[8,16,64,128]{3,2,1,0:T(8,128)} custom-call(f32[2,64,128,512]{3,2,1,0:T(8,128)} %k_ref.13, f32[128,512]{1,0:T(8,128)S(1)} %bitcast.65, f32[8,16,64,128]{3,2,1,0:T(8,128)} %second.3.refs_1_), custom_call_target="tpu_custom_call", output_to_operand_aliasing={{}: (2, {})} | custom-call | flops 1610612 | bytes 10485 | tf_op jit(solution)/shard_map/second/pallas_call | solution.py:89
  36.2 5.8 %all-to-all-start = ((f32[8,16,64,128]{3,2,1,0:T(8,128)}), f32[8,16,64,128]{3,2,1,0:T(8,128)}, u32[]{:S(2)}, u32[]{:S(2)}) async-start(f32[8,16,64,128]{3,2,1,0:T(8,128)} %second.4), calls=%async_computation | async-start | bytes 8388608 | tf_op jit(solution)/shard_map/all_to_all | solution.py:286
  42.1 1.6 collective-permute-start.8
  43.6 15.9 %collective-permute-done.8 = f32[3,512,128]{2,1,0:T(8,128)S(1)} collective-permute-done((f32[3,512,128]{2,1,0:T(8,128)S(1)}, f32[3,512,128]{2,1,0:T(8,128)S(1)}, u32[]{:S(2)}, u32[]{:S(2)}) %collective-permute-start.8) | collective-permute-done | bytes 786464 | tf_op jit(solution)/shard_map/ppermute | solution.py:283
  59.5 0.3 fusion.1
  59.9 3.5 collective-permute-done.9
  63.4 1.6 pad_maximum_fusion
  65.2 0.2 dynamic-slice_bitcast_fusion.3
  65.7 0.3 fusion.2
  66.0 0.9 slice.41
  66.9 1.2 reshape.50.refs_0_
  68.3 23.2 %third.1 = (f32[64,128,128]{2,1,0:T(8,128)}, f32[64,128,128]{2,1,0:T(8,128)}, f32[64,128,128]{2,1,0:T(8,128)}, f32[64,128,128]{2,1,0:T(8,128)}) custom-call(f32[2,64,128,512]{3,2,1,0:T(8,128)} %k_ref.13, f32[512,512]{1,0:T(8,128)S(1)} %pad_maximum_fusion.3.d_ref), custom_call_target="tpu_custom_call" | custom-call | flops 12884901 | bytes 33554 | tf_op jit(solution)/shard_map/third/pallas_call | solution.py:133
  91.5 21.2 %second.5 = (f32[8,44,64,128]{3,2,1,0:T(8,128)}, f32[8,4,64,128]{3,2,1,0:T(8,128)}) custom-call(f32[2,64,128,512]{3,2,1,0:T(8,128)} %k_ref.13, f32[352,512]{1,0:T(8,128)S(1)} %reshape.50.refs_0_, f32[32,512]{1,0:T(8,128)S(1)} %reshape.51.refs_1_), custom_call_target="tpu_custom_call" | custom-call | flops 9663676 | bytes 29360 | tf_op jit(solution)/shard_map/second/pallas_call | solution.py:89
  112.7 20.9 %all-to-all-done.t_ref = f32[8,16,64,128]{3,2,1,0:T(8,128)} async-done(((f32[8,16,64,128]{3,2,1,0:T(8,128)}), f32[8,16,64,128]{3,2,1,0:T(8,128)}, u32[]{:S(2)}, u32[]{:S(2)}) %all-to-all-start) | async-done | bytes 4194336 | tf_op jit(solution)/shard_map/all_to_all | solution.py:286
  133.6 5.4 %all-to-all-start.1 = ((f32[8,44,64,128]{3,2,1,0:T(8,128)}), f32[8,44,64,128]{3,2,1,0:T(8,128)}, u32[]{:S(2)}, u32[]{:S(2)}) async-start(f32[8,44,64,128]{3,2,1,0:T(8,128)} %get-tuple-element.36), calls=%async_computation.1 | async-start | bytes 23068672 | tf_op jit(solution)/shard_map/all_to_all | solution.py:286
  139.1 1.6 collective-permute-start.11
  140.7 0.3 collective-permute-start.12
  141.0 0.2 select_reduce_fusion
  141.3 0.7 select_reduce_fusion.1
  142.0 0.7 dynamic-slice_subtract_fusion.eb_ref
  142.8 3.8 collective-permute-done.10.refs_1_
  146.6 86.3 %collective-permute-done.11.refs_2_ = f32[64,128,128]{2,1,0:T(8,128)} collective-permute-done((f32[64,128,128]{2,1,0:T(8,128)}, f32[64,128,128]{2,1,0:T(8,128)}, u32[]{:S(2)}, u32[]{:S(2)}) %collective-permute-start.11) | collective-permute-done | bytes 4194336 | tf_op jit(solution)/shard_map/ppermute | solution.py:283
  232.9 89.0 %collective-permute-done.12.refs_3_ = f32[64,128,128]{2,1,0:T(8,128)} collective-permute-done((f32[64,128,128]{2,1,0:T(8,128)}, f32[64,128,128]{2,1,0:T(8,128)}, u32[]{:S(2)}, u32[]{:S(2)}) %collective-permute-start.12) | collective-permute-done | bytes 4194336 | tf_op jit(solution)/shard_map/ppermute | solution.py:283
  321.9 2.2 copy-done
  324.1 26.7 %first.1.q_ref = f32[64,512,128]{2,1,0:T(8,128)} custom-call(s32[4]{0:T(128)S(1)} %pad_add_fusion.off_ref, f32[2,64,128,512]{3,2,1,0:T(8,128)} %k_ref.13, f32[512,512]{1,0:T(8,128)S(1)} %get-tuple-element.46.d_ref, f32[64,128,128]{2,1,0:T(8,128)S(1)} %copy-done, f32[64,128,128]{2,1,0:T(8,128)} %collective-permute-done.10.refs_1_, ...), custom_call_target="tpu_custom_call" | custom-call | flops 12884901 | bytes 50331 | tf_op jit(solution)/shard_map/first/pallas_call | solution.py:178
  350.9 9.5 %finish.3 = (f32[64,128,512]{2,1,0:T(8,128)}, f32[4,512,128]{2,1,0:T(8,128)}) custom-call(f32[64]{0:T(128)S(1)} %dynamic-slice_subtract_fusion.eb_ref, f32[1,128]{1,0:T(1,128)S(1)} %dynamic-slice_bitcast_fusion.9.ec_ref, f32[512,128]{1,0:T(8,128)S(1)} %broadcast_in_dim.44.ea_ref, f32[2,64,128,512]{3,2,1,0:T(8,128)} %k_ref.13, f32[64,512,128]{2,1,0:T(8,128)} %first.1.q_ref, ...), custom_call_target="tpu_custom_call" | custom-call | flops 3221225 | bytes 16777 | tf_op jit(solution)/shard_map/finish/pallas_call | solution.py:228
  360.4 27.7 %all-to-all-done.1.t_ref = f32[8,44,64,128]{3,2,1,0:T(8,128)} async-done(((f32[8,44,64,128]{3,2,1,0:T(8,128)}), f32[8,44,64,128]{3,2,1,0:T(8,128)}, u32[]{:S(2)}, u32[]{:S(2)}) %all-to-all-start.1) | async-done | bytes 11534368 | tf_op jit(solution)/shard_map/all_to_all | solution.py:286
  388.2 4.0 all-to-all-start.2
  392.2 23.3 %finish.4 = (f32[64,128,512]{2,1,0:T(8,128)}, f32[4,512,128]{2,1,0:T(8,128)}) custom-call(f32[64]{0:T(128)S(1)} %dynamic-slice_subtract_fusion.eb_ref, f32[1,128]{1,0:T(1,128)S(1)} %dynamic-slice_bitcast_fusion.9.ec_ref, f32[512,128]{1,0:T(8,128)S(1)} %broadcast_in_dim.44.ea_ref, ...), custom_call_target="tpu_custom_call", output_to_operand_aliasing={{0}: (6, {}), {1}: (7, {})} | custom-call | flops 8858370 | bytes 46137 | tf_op jit(solution)/shard_map/finish/pallas_call | solution.py:228
  415.5 2.6 all-to-all-done.2.t_ref
  418.2 4.7 %finish.5 = (f32[64,128,512]{2,1,0:T(8,128)}, f32[4,512,128]{2,1,0:T(8,128)}) custom-call(f32[64]{0:T(128)S(1)} %dynamic-slice_subtract_fusion.eb_ref, f32[1,128]{1,0:T(1,128)S(1)} %dynamic-slice_bitcast_fusion.9.ec_ref, f32[512,128]{1,0:T(8,128)S(1)} %broadcast_in_dim.44.ea_ref, ...), custom_call_target="tpu_custom_call", output_to_operand_aliasing={{0}: (6, {}), {1}: (7, {})} | custom-call | flops 805306 | bytes 4194 | tf_op jit(solution)/shard_map/finish/pallas_call | solution.py:228
  422.9 1.1 dynamic-slice_bitcast_fusion.4
  424.1 1.9 collective-permute-done.13
  425.9 1.1 bitcast_add_fusion
  427.1 19.9 %all_to_all.20 = f32[16,64,128]{2,1,0:T(8,128)S(1)} all-to-all(f32[16,64,128]{2,1,0:T(8,128)S(1)} %bitcast.82), channel_id=1, replica_groups={{0,2,4,6,8,10,12,14,16,18,20,22,24,26,28,30},{1,3,5,7,9,11,13,15,17,19,..., dimensions={0} | all-to-all | bytes 1048576 | tf_op jit(solution)/shard_map/all_to_all | solution.py:360
  446.9 0.6 reduce_sum.29
  (51 shorter events, 1.7 us)
Async XLA Ops:
  1.4 10.9 %collective-permute-start.5 = (f32[16,512]{1,0:T(8,128)S(1)}, f32[16,512]{1,0:T(8,128)S(1)}, u32[]{:S(2)}, u32[]{:S(2)}) collective-permute-start(f32[16,512]{1,0:T(8,128)S(1)} %get-tuple-element.58), channel_id=1, source_target_pairs={{0,24},{4,28},{8,16},{12,20},{16,8},{20,12},{24,0},{28,4},{1,25},{... | collective-permute-start | bytes 98312 | tf_op jit(solution)/shard_map/ppermute | solution.py:280
  6.4 5.9 %collective-permute-start.4 = (f32[16,512]{1,0:T(8,128)S(1)}, f32[16,512]{1,0:T(8,128)S(1)}, u32[]{:S(2)}, u32[]{:S(2)}) collective-permute-start(f32[16,512]{1,0:T(8,128)S(1)} %get-tuple-element.58), channel_id=1, source_target_pairs={{0,16},{4,20},{8,24},{12,28},{16,0},{20,4},{24,8},{28,12},{1,17},{... | collective-permute-start | bytes 98312 | tf_op jit(solution)/shard_map/ppermute | solution.py:280
  6.4 5.9 %collective-permute-start.3 = (f32[16,512]{1,0:T(8,128)S(1)}, f32[16,512]{1,0:T(8,128)S(1)}, u32[]{:S(2)}, u32[]{:S(2)}) collective-permute-start(f32[16,512]{1,0:T(8,128)S(1)} %get-tuple-element.58), channel_id=1, source_target_pairs={{0,8},{4,12},{8,0},{12,4},{16,24},{20,28},{24,16},{28,20},{1,9},{5... | collective-permute-start | bytes 98312 | tf_op jit(solution)/shard_map/ppermute | solution.py:280
  7.9 8.8 %collective-permute-start.1 = (f32[3,64,128]{2,1,0:T(8,128)S(1)}, f32[3,64,128]{2,1,0:T(8,128)S(1)}, u32[]{:S(2)}, u32[]{:S(2)}) collective-permute-start(f32[3,64,128]{2,1,0:T(8,128)S(1)} %constant_dynamic-slice_fusion), channel_id=1, source_target_pairs={{0,16},{4,20},{8,24},{12,28},{16,0},{20,4},{24,8},{28,12},{1,17},{... | collective-permute-start | bytes 294920 | tf_op jit(solution)/shard_map/ppermute | solution.py:280
  10.3 6.4 %collective-permute-start = (f32[3,64,128]{2,1,0:T(8,128)S(1)}, f32[3,64,128]{2,1,0:T(8,128)S(1)}, u32[]{:S(2)}, u32[]{:S(2)}) collective-permute-start(f32[3,64,128]{2,1,0:T(8,128)S(1)} %constant_dynamic-slice_fusion), channel_id=1, source_target_pairs={{0,8},{4,12},{8,0},{12,4},{16,24},{20,28},{24,16},{28,20},{1,9},{5... | collective-permute-start | bytes 294920 | tf_op jit(solution)/shard_map/ppermute | solution.py:280
  12.3 6.5 %collective-permute-start.2 = (f32[3,64,128]{2,1,0:T(8,128)S(1)}, f32[3,64,128]{2,1,0:T(8,128)S(1)}, u32[]{:S(2)}, u32[]{:S(2)}) collective-permute-start(f32[3,64,128]{2,1,0:T(8,128)S(1)} %constant_dynamic-slice_fusion), channel_id=1, source_target_pairs={{0,24},{4,28},{8,16},{12,20},{16,8},{20,12},{24,0},{28,4},{1,25},{... | collective-permute-start | bytes 294920 | tf_op jit(solution)/shard_map/ppermute | solution.py:280
  12.3 6.5 %collective-permute-start.6 = (f32[4,16,512]{2,1,0:T(8,128)S(1)}, f32[4,16,512]{2,1,0:T(8,128)S(1)}, u32[]{:S(2)}, u32[]{:S(2)}) collective-permute-start(f32[4,16,512]{2,1,0:T(8,128)S(1)} %get-tuple-element.60), channel_id=1, source_target_pairs={{0,4},{4,0},{8,12},{12,8},{16,20},{20,16},{24,28},{28,24},{1,5},{5... | collective-permute-start | bytes 393224 | tf_op jit(solution)/shard_map/ppermute | solution.py:280
  26.7 9.2 %collective-permute-start.7 = (f32[4,3,64,128]{3,2,1,0:T(8,128)S(1)}, f32[4,3,64,128]{3,2,1,0:T(8,128)S(1)}, u32[]{:S(2)}, u32[]{:S(2)}) collective-permute-start(f32[4,3,64,128]{3,2,1,0:T(8,128)S(1)} %pad_maximum_fusion.5), channel_id=1, source_target_pairs={{0,4},{4,0},{8,12},{12,8},{16,20},{20,16},{24,28},{28,24},{1,5},{5... | collective-permute-start | bytes 1179656 | tf_op jit(solution)/shard_map/ppermute | solution.py:280
  36.2 97.4 %all-to-all-start = ((f32[8,16,64,128]{3,2,1,0:T(8,128)}), f32[8,16,64,128]{3,2,1,0:T(8,128)}, u32[]{:S(2)}, u32[]{:S(2)}) async-start(f32[8,16,64,128]{3,2,1,0:T(8,128)} %second.4), calls=%async_computation | async-start | bytes 8388608 | tf_op jit(solution)/shard_map/all_to_all | solution.py:286
  42.1 17.4 %collective-permute-start.8 = (f32[3,512,128]{2,1,0:T(8,128)S(1)}, f32[3,512,128]{2,1,0:T(8,128)S(1)}, u32[]{:S(2)}, u32[]{:S(2)}) collective-permute-start(f32[3,512,128]{2,1,0:T(8,128)S(1)} %bitcast.79), channel_id=1, source_target_pairs={{0,2},{1,3},{2,0},{3,1},{4,6},{5,7},{6,4},{7,5},{8,10},{9,11},{10,... | collective-permute-start | bytes 2359304 | tf_op jit(solution)/shard_map/ppermute | solution.py:283
  59.8 3.6 collective-permute-start.9
  133.6 7.4 %copy-start.1 = (f32[512]{0:T(512)S(1)}, f32[512]{0:T(512)}, u32[]{:S(2)}) copy-start(f32[512]{0:T(512)} %param.9) | copy-start | bytes 6148
  133.6 7.4 %copy-start.2 = (s32[512]{0:T(512)S(1)}, s32[512]{0:T(512)}, u32[]{:S(2)}) copy-start(s32[512]{0:T(512)} %param.11) | copy-start | bytes 6148
  133.6 7.7 %copy-start.3 = (f32[100]{0:T(128)S(1)}, f32[100]{0:T(128)}, u32[]{:S(2)}) copy-start(f32[100]{0:T(128)} %param.8) | copy-start | bytes 1204
  133.6 7.7 %copy-start.4 = (s32[3]{0:T(128)S(1)}, s32[3]{0:T(128)}, u32[]{:S(2)}) copy-start(s32[3]{0:T(128)} %param.10) | copy-start | bytes 40
  133.6 254.5 %all-to-all-start.1 = ((f32[8,44,64,128]{3,2,1,0:T(8,128)}), f32[8,44,64,128]{3,2,1,0:T(8,128)}, u32[]{:S(2)}, u32[]{:S(2)}) async-start(f32[8,44,64,128]{3,2,1,0:T(8,128)} %get-tuple-element.36), calls=%async_computation.1 | async-start | bytes 23068672 | tf_op jit(solution)/shard_map/all_to_all | solution.py:286
  139.1 7.6 %collective-permute-start.10 = (f32[64,128,128]{2,1,0:T(8,128)}, f32[64,128,128]{2,1,0:T(8,128)}, u32[]{:S(2)}, u32[]{:S(2)}) collective-permute-start(f32[64,128,128]{2,1,0:T(8,128)} %get-tuple-element.27), channel_id=1, source_target_pairs={{0,1},{1,0},{2,3},{3,2},{4,5},{5,4},{6,7},{7,6},{8,9},{9,8},{10,11... | collective-permute-start | bytes 12582920 | tf_op jit(solution)/shard_map/ppermute | solution.py:283
  139.1 93.8 %collective-permute-start.11 = (f32[64,128,128]{2,1,0:T(8,128)}, f32[64,128,128]{2,1,0:T(8,128)}, u32[]{:S(2)}, u32[]{:S(2)}) collective-permute-start(f32[64,128,128]{2,1,0:T(8,128)} %get-tuple-element.28), channel_id=1, source_target_pairs={{0,2},{1,3},{2,0},{3,1},{4,6},{5,7},{6,4},{7,5},{8,10},{9,11},{10,... | collective-permute-start | bytes 12582920 | tf_op jit(solution)/shard_map/ppermute | solution.py:283
  140.7 181.2 %collective-permute-start.12 = (f32[64,128,128]{2,1,0:T(8,128)}, f32[64,128,128]{2,1,0:T(8,128)}, u32[]{:S(2)}, u32[]{:S(2)}) collective-permute-start(f32[64,128,128]{2,1,0:T(8,128)} %get-tuple-element.29), channel_id=1, source_target_pairs={{0,3},{1,2},{2,1},{3,0},{4,7},{5,6},{6,5},{7,4},{8,11},{9,10},{10,... | collective-permute-start | bytes 12582920 | tf_op jit(solution)/shard_map/ppermute | solution.py:283
  321.9 2.2 copy-start
  388.2 30.0 %all-to-all-start.2 = ((f32[8,4,64,128]{3,2,1,0:T(8,128)}), f32[8,4,64,128]{3,2,1,0:T(8,128)S(1)}, u32[]{:S(2)}, u32[]{:S(2)}) async-start(f32[8,4,64,128]{3,2,1,0:T(8,128)} %get-tuple-element.38), calls=%async_computation.2 | async-start | bytes 2097152 | tf_op jit(solution)/shard_map/all_to_all | solution.py:286
  424.0 2.0 collective-permute-start.13
